TPU v7x, 256 devices: a whole 4x4x8 slice. The times are simulated.
256 devices in a mesh: level: 2 (over x_lo), row: 16 (over z, core), col: 8 (over y, x_hi).
Axes of the slice: x: 4 (x_hi: 2, x_lo: 2; x = x_hi * 2 + x_lo), y: 4, z: 8, core: 2. Of those that a mesh axis runs over, the one named last changes fastest.
Arguments:
- noise: bfloat16 [64, 512, 512], P('row', ('level', 'col')), may hold values from -6 to 6
- source: bfloat16 [64, 512, 512], P('row', ('level', 'col')), may hold values from -16 to 16
Outputs:
- fine_pressure: float32 [64, 512, 512], P('row', ('level', 'col'))
- coarse_pressure: float32 [32, 256, 256], P('row', ('level', 'col'))
All inputs are finite; a program needn't handle non-finite values.
Results may differ from a plain program's by a relative error of at most 0.00035.
Values sent between devices are 32-bit elements; how exact they have to be, the bound alone decides.
A program may use at most 128 MiB of HBM per device.

v0:
```python
import functools
import math

import jax
import jax.numpy as jnp
import ml_dtypes
import numpy as np
from jax import lax
from jax.experimental import pallas as pl
from jax.experimental.pallas import tpu as pltpu
from jax.sharding import PartitionSpec as P

JACOBI_WEIGHT = 2.0 / 3.0
CORRELATION = 0.2
FIELD_SCALE = 0.3
LOGICAL = pl.DeviceIdType.LOGICAL
F32 = jnp.float32
BF16 = jnp.bfloat16

N0, N1, N2 = 64, 512, 512
ROWS, COLS = 16, 16
DEVICES = ROWS * COLS
PB, QB = N0 // ROWS, N1 // COLS
LANES = PB * QB
EDGE = 8


def split_table(table):
    high = table.astype(ml_dtypes.bfloat16)
    low = (table - high.astype(np.float64)).astype(ml_dtypes.bfloat16)
    return high, low


def signed(index, length):
    return np.where(index < length // 2, index, index - length).astype(np.float64)


@functools.lru_cache(maxsize=None)
def tables():
    place = np.arange(DEVICES)
    r, c = place // COLS, place % COLS
    third = (r % 2) * 128 + (r // 2) * 16 + c
    turn = 2.0 * np.pi
    n2 = np.arange(N2)
    angle = turn * ((third[:, None] * n2[None, :]) % N2) / N2
    third_table = np.stack([np.cos(angle), -np.sin(angle)], axis=1).reshape(2 * DEVICES, N2)
    k2 = np.arange(128)
    angle = turn * ((k2[:, None] * np.arange(N2 // 2)[None, :]) % (N2 // 2)) / (N2 // 2)
    coarse_third = np.concatenate([np.cos(angle), -np.sin(angle)], axis=0)
    a, b = place // 16, place % 16
    angle = turn * ((a[:, None] * r[None, :] + b[:, None] * c[None, :]) % 16) / 16
    cos, sin = np.cos(angle), np.sin(angle)
    outer = np.concatenate([np.stack([cos, sin], axis=2), np.stack([-sin, cos], axis=2)], axis=0)
    outer = outer.reshape(2 * DEVICES, 2 * DEVICES)
    lane = np.arange(LANES)
    p, q = lane // QB, lane % QB
    angle = turn * (((8 * p[:, None] * p[None, :]) + q[:, None] * q[None, :]) % 32) / 32
    cos, sin = np.cos(angle), np.sin(angle)
    inner = np.block([[cos, -sin], [sin, cos]])
    lane_c = np.arange(32)
    pc, qc = lane_c // 16, lane_c % 16
    angle = turn * (((8 * p[:, None] * pc[None, :]) + q[:, None] * qc[None, :]) % 16) / 16
    cos, sin = np.cos(angle), np.sin(angle)
    empty = np.zeros((LANES, LANES - 64))
    inner_c = np.block([[cos, cos, empty, sin, sin, empty], [-sin, -sin, empty, cos, cos, empty]])
    angle = turn * ((8 * a[:, None] * p[None, :] + b[:, None] * q[None, :]) % 512) / 512
    twist = np.stack([np.cos(angle), np.sin(angle)])
    angle = turn * ((8 * a[:, None] * pc[None, :] + b[:, None] * qc[None, :]) % 256) / 256
    cos, sin = np.cos(angle), np.sin(angle)
    rest = np.zeros((DEVICES, LANES - 64))
    twist_c = np.stack([np.concatenate([cos, sin, rest], 1), np.concatenate([sin, -cos, rest], 1)])
    m0 = signed(a[:, None] + 16 * p[None, :], N0)
    m1 = signed(b[:, None] + 16 * q[None, :], N1)
    norm = (float(N0) * N1 * N2) ** -0.5
    inside = (m0 != -N0 // 2) & (m1 != -N1 // 2)
    inside_c = (np.abs(m0) < N0 // 4) & (np.abs(m1) < N1 // 4)
    waves = np.stack([m0 * m0 + m1 * m1, inside * FIELD_SCALE * norm, inside_c * FIELD_SCALE * norm])
    pool = (np.arange(N2)[:, None] // 2 == np.arange(N2 // 2)[None, :]).astype(ml_dtypes.bfloat16)
    pool_rows = (lane_c[:, None] == ((p // 2) * 16 + q // 2)[None, :]) * 0.125
    return (
        np.stack(split_table(third_table)),
        np.stack(split_table(outer)),
        np.stack(split_table(outer.T)),
        np.stack(split_table(inner)),
        np.stack(split_table(inner.T)),
        np.stack(split_table(inner_c)),
        np.stack(split_table(coarse_third)),
        pool,
        pool_rows.astype(ml_dtypes.bfloat16),
        twist.astype(np.float32),
        twist_c.astype(np.float32),
        waves.astype(np.float32),
    )


def halves(value):
    high = value.astype(BF16)
    return high, (value - high.astype(F32)).astype(BF16)


def dot(left, right):
    return jnp.dot(left, right, preferred_element_type=F32)


def table_left(table, value):
    high, low = halves(value)
    width = value.shape[1]
    both = dot(table[0], jnp.concatenate([high, low], axis=1))
    return both[:, :width] + (both[:, width:] + dot(table[1], high))


def table_right(value, table):
    high, low = halves(value)
    return dot(high, table[0]) + (dot(high, table[1]) + dot(low, table[0]))


DIRECTIONS = ((-1, 0), (1, 0), (0, -1), (0, 1), (-1, -1), (-1, 1), (1, -1), (1, 1))
OPPOSITE = (1, 0, 3, 2, 7, 6, 5, 4)


def flat_id(r, c):
    return (c // 8) * 128 + r * 8 + c % 8


def face_weight(center, beside):
    return jnp.where(beside > 0.0, 0.5 * (center + beside), center)


def smooth(kappa, source, first, out, planes, width, depth):
    tall = width + 2 * EDGE
    lane = lax.broadcasted_iota(jnp.int32, (tall, depth), 1)
    lane_in = lax.broadcasted_iota(jnp.int32, (width, depth), 1)
    diagonals = []
    for plane in range(planes + 2):
        center = kappa[plane + 1]
        diagonal = face_weight(center, kappa[plane + 2])
        diagonal = diagonal + face_weight(center, kappa[plane])
        diagonal = diagonal + face_weight(center, pltpu.roll(center, tall - 1, 0))
        diagonal = diagonal + face_weight(center, pltpu.roll(center, 1, 0))
        after = jnp.where(lane == depth - 1, 0.0, pltpu.roll(center, depth - 1, 1))
        before = jnp.where(lane == 0, 0.0, pltpu.roll(center, 1, 1))
        diagonal = diagonal + face_weight(center, after) + face_weight(center, before)
        guarded = jnp.where(center > 0.0, diagonal, 1.0)
        first[plane] = JACOBI_WEIGHT * source[plane] / guarded
    mid, low, high = pl.ds(EDGE, width), pl.ds(EDGE - 1, width), pl.ds(EDGE + 1, width)
    for plane in range(planes):
        center = kappa[plane + 2, mid]
        inner = first[plane + 1, mid]
        total = jnp.zeros_like(center)
        diagonal = jnp.zeros_like(center)
        for beside, value in (
            (kappa[plane + 3, mid], first[plane + 2, mid]),
            (kappa[plane + 1, mid], first[plane, mid]),
            (kappa[plane + 2, high], first[plane + 1, high]),
            (kappa[plane + 2, low], first[plane + 1, low]),
        ):
            face = face_weight(center, beside)
            diagonal = diagonal + face
            total = total + face * value
        for shift, missing in ((depth - 1, depth - 1), (1, 0)):
            outside = lane_in == missing
            beside = jnp.where(outside, 0.0, pltpu.roll(center, shift, 1))
            value = jnp.where(outside, 0.0, pltpu.roll(inner, shift, 1))
            face = face_weight(center, beside)
            diagonal = diagonal + face
            total = total + face * value
        residual = source[plane + 1, mid] - diagonal * inner + total
        out[plane] = inner + JACOBI_WEIGHT * residual / diagonal


def kernel(
    noise, source, third_h, outer_h, outer_t_h, inner_h, inner_t_h, inner_c_h, coarse_third_h, pool_h, pool_rows_h, twist_h, twist_c_h,
    waves_h, fine_out, coarse_out,
    third_t, outer, outer_t, inner, inner_t, inner_c, coarse_third, pool, pool_rows, twist, twist_c, waves,
    send_f, recv_f, send_i, recv_i, send_c, recv_c,
    ke, fe, ue, kc, fc, uc,
    col_s, col_r, ccol_s, ccol_r, cor_s, cor_r, ccor_s, ccor_r, scol_s, scol_r, cscol_s, cscol_r,
    table_sem, fwd_sem, inv_sem, crs_sem, own_sem, halo_s, halo_r, chalo_s, chalo_r, src_s, src_r, csrc_s, csrc_r,
):
    level, row, col = lax.axis_index("level"), lax.axis_index("row"), lax.axis_index("col")
    group = level * 8 + col
    me = flat_id(row, group)
    place = row * COLS + group
    core = row % 2

    for ref in (ke, fe, kc, fc):
        ref[...] = jnp.zeros_like(ref)

    barrier = pltpu.get_barrier_semaphore()

    def greet(i, carry):
        pl.semaphore_signal(barrier, inc=1, device_id=(me + i) % DEVICES, device_id_type=LOGICAL)
        return carry

    lax.fori_loop(1, DEVICES, greet, 0, unroll=15)

    pairs = (
        (third_h, third_t), (pool_h, pool), (pool_rows_h, pool_rows), (outer_h, outer), (twist_h, twist), (inner_h, inner), (waves_h, waves),
        (inner_t_h, inner_t), (inner_c_h, inner_c), (twist_c_h, twist_c), (outer_t_h, outer_t),
        (coarse_third_h, coarse_third),
    )
    loads = [pltpu.make_async_copy(a, b, table_sem.at[i]) for i, (a, b) in enumerate(pairs)]
    for load in loads:
        load.start()

    fe[pl.ds(1, PB), pl.ds(EDGE, QB)] = source[...].astype(F32)
    scol_s[0, :, 0] = source[:, 0].astype(F32)
    scol_s[1, :, 0] = source[:, QB - 1].astype(F32)
    loads[0].wait()
    noise_rows = noise[...].reshape(LANES, N2)
    contract = (((1,), (1,)), ((), ()))
    spectrum = lax.dot_general(third_t[0], noise_rows, contract, preferred_element_type=F32)
    spectrum = spectrum + lax.dot_general(third_t[1], noise_rows, contract, preferred_element_type=F32)
    send_f[...] = spectrum.reshape(DEVICES, 2, LANES)
    loads[1].wait()
    loads[2].wait()
    high, low = halves(dot(pool_rows[...], source[...].reshape(LANES, N2)))
    pooled = (dot(high, pool[...]) + dot(low, pool[...])).reshape(PB // 2, QB // 2, N2 // 2)
    fc[pl.ds(1, PB // 2), pl.ds(EDGE, QB // 2)] = pooled
    cscol_s[0, :, 0] = pooled[:, 0]
    cscol_s[1, :, 0] = pooled[:, QB // 2 - 1]

    pl.semaphore_wait(barrier, DEVICES - 1)

    def peer_at(i):
        j = i // 32
        half = (j + 1) // 2
        z = (row // 2 + 4 + jnp.where(j % 2 == 1, -half, half)) % 8
        k = 31 - i % 32
        r = z * 2 + (core + k // 16) % 2
        y = (col // 2 + (k // 4) % 4) % 4
        x = ((col % 2) * 2 + level + k % 4) % 4
        c = (x % 2) * 8 + y * 2 + x // 2
        return r, c

    def push(i, carry):
        r, c = peer_at(i)
        pltpu.make_async_remote_copy(
            src_ref=send_f.at[r * COLS + c], dst_ref=recv_f.at[place], send_sem=fwd_sem.at[0], recv_sem=fwd_sem.at[1],
            device_id=flat_id(r, c), device_id_type=LOGICAL,
        ).start()
        return carry

    lax.fori_loop(0, DEVICES - 1, push, 0, unroll=15)
    recv_f[place] = send_f[place]

    def neighbour(d):
        dr, dc = DIRECTIONS[d]
        r, c = row + dr, group + dc
        exists = (r >= 0) & (r < ROWS) & (c >= 0) & (c < COLS)
        return exists, flat_id(r, c)

    def halo_copies(d, kind):
        half_p, half_q = PB // 2, QB // 2
        mid, mid_c = pl.ds(EDGE, QB), pl.ds(EDGE, half_q)
        back = OPPOSITE[d]
        if kind == "source":
            if d < 2:
                here = (fe.at[1 if d == 0 else PB, mid], fe.at[PB + 1 if d == 0 else 0, mid], fe.at[0 if d == 0 else PB + 1, mid])
                there = (
                    fc.at[1 if d == 0 else half_p, mid_c], fc.at[half_p + 1 if d == 0 else 0, mid_c],
                    fc.at[0 if d == 0 else half_p + 1, mid_c],
                )
                return ((*here, src_s, src_r), (*there, csrc_s, csrc_r))
            return (
                (scol_s.at[d - 2], scol_r.at[back - 2], scol_r.at[d - 2], src_s, src_r),
                (cscol_s.at[d - 2], cscol_r.at[back - 2], cscol_r.at[d - 2], csrc_s, csrc_r),
            )
        if d < 2:
            return (
                (
                    ke.at[pl.ds(2 if d == 0 else PB, 2), mid], ke.at[pl.ds(PB + 2 if d == 0 else 0, 2), mid],
                    ke.at[pl.ds(0 if d == 0 else PB + 2, 2), mid], halo_s, halo_r,
                ),
                (
                    kc.at[pl.ds(2, 2), mid_c], kc.at[pl.ds(half_p + 2 if d == 0 else 0, 2), mid_c],
                    kc.at[pl.ds(0 if d == 0 else half_p + 2, 2), mid_c], chalo_s, chalo_r,
                ),
            )
        if d < 4:
            return (
                (col_s.at[d - 2], col_r.at[back - 2], col_r.at[d - 2], halo_s, halo_r),
                (ccol_s.at[d - 2], ccol_r.at[back - 2], ccol_r.at[d - 2], chalo_s, chalo_r),
            )
        return (
            (cor_s.at[d - 4], cor_r.at[back - 4], cor_r.at[d - 4], halo_s, halo_r),
            (ccor_s.at[d - 4], ccor_r.at[back - 4], ccor_r.at[d - 4], chalo_s, chalo_r),
        )

    def halo_start(d, kind, which):
        exists, there = neighbour(d)
        src, dst, _, s_sem, r_sem = halo_copies(d, kind)[which]

        @pl.when(exists)
        def _():
            pltpu.make_async_remote_copy(
                src_ref=src, dst_ref=dst, send_sem=s_sem.at[d], recv_sem=r_sem.at[OPPOSITE[d]], device_id=there,
                device_id_type=LOGICAL,
            ).start()

    def halo_wait(d, kind, which, then):
        exists, there = neighbour(d)
        src, _, here, s_sem, r_sem = halo_copies(d, kind)[which]

        @pl.when(exists)
        def _():
            copy = pltpu.make_async_remote_copy(
                src_ref=src, dst_ref=here, send_sem=s_sem.at[d], recv_sem=r_sem.at[d], device_id=there,
                device_id_type=LOGICAL,
            )
            copy.wait_send()
            copy.wait_recv()
            if then is not None:
                then()

    for d in range(4):
        for which in range(2):
            halo_start(d, "source", which)
    for load in loads[3:]:
        load.wait()

    many = pl.ds(0, DEVICES - 1)
    arrived = pltpu.make_async_remote_copy(
        src_ref=send_f.at[many], dst_ref=recv_f.at[many], send_sem=fwd_sem.at[0], recv_sem=fwd_sem.at[1], device_id=me,
        device_id_type=LOGICAL,
    )
    arrived.wait_recv()

    z = table_left(outer, recv_f[...].reshape(2 * DEVICES, LANES))
    z_re, z_im = z[:DEVICES], z[DEVICES:]
    turned = jnp.concatenate([z_re * twist[0] + z_im * twist[1], z_im * twist[0] - z_re * twist[1]], axis=1)
    y = table_right(turned, inner)
    third = core * 128 + (row // 2) * 16 + group
    third_f = third.astype(F32)
    weight = jnp.where(third == 0, 1.0, 2.0)
    damp = weight / (1.0 + (2.0 * math.pi * CORRELATION) ** 2 * (waves[0] + third_f * third_f))
    amp = waves[1] * damp
    amp_c = waves[2] * damp
    x = table_right(y * jnp.concatenate([amp, amp], axis=1), inner_t)
    x_re, x_im = x[:, :LANES], x[:, LANES:]
    xc = table_right(y * jnp.concatenate([amp_c, amp_c], axis=1), inner_c)
    xc_re, xc_im = xc[:, :LANES], xc[:, LANES:]
    fine_part = jnp.concatenate([x_re * twist[0] - x_im * twist[1], x_im * twist[0] + x_re * twist[1]], axis=0)
    coarse_part = jnp.concatenate(
        [xc_re * twist_c[0] - xc_im * twist_c[1], xc_im * twist_c[0] + xc_re * twist_c[1]], axis=0
    )
    both = jnp.concatenate([fine_part, coarse_part], axis=1)
    high, low = halves(both)
    planes = dot(outer_t[0], high) + (dot(outer_t[0], low) + dot(outer_t[1], high))
    send_i[...] = planes[:, :LANES].reshape(DEVICES, 2, LANES)
    send_c[...] = planes[:, LANES:].reshape(DEVICES, 2, LANES)[:, 0:1, :]

    def push_back(i, carry):
        r, c = peer_at(i)
        pltpu.make_async_remote_copy(
            src_ref=send_i.at[r * COLS + c], dst_ref=recv_i.at[place], send_sem=inv_sem.at[0], recv_sem=inv_sem.at[1],
            device_id=flat_id(r, c), device_id_type=LOGICAL,
        ).start()
        return carry

    def push_coarse(i, carry):
        r, c = peer_at(i)
        pltpu.make_async_remote_copy(
            src_ref=send_c.at[r * COLS + c], dst_ref=recv_c.at[(row // 2) * COLS + group], send_sem=crs_sem.at[0],
            recv_sem=crs_sem.at[1], device_id=flat_id(r, c), device_id_type=LOGICAL,
        ).start()
        return carry

    lax.fori_loop(0, DEVICES - 1, push_back, 0, unroll=15)
    recv_i[place] = send_i[place]

    @pl.when(core == 0)
    def _():
        lax.fori_loop(0, DEVICES - 1, push_coarse, 0, unroll=15)
        recv_c[(row // 2) * COLS + group] = send_c[place]

    back = pltpu.make_async_remote_copy(
        src_ref=send_i.at[many], dst_ref=recv_i.at[many], send_sem=inv_sem.at[0], recv_sem=inv_sem.at[1], device_id=me,
        device_id_type=LOGICAL,
    )
    back.wait_recv()
    field = recv_i[...].reshape(2 * DEVICES, LANES)
    fine_log = table_right(field.T, third_t)
    fine_kappa = jnp.exp(fine_log).reshape(PB, QB, N2)
    ke[pl.ds(2, PB), pl.ds(EDGE, QB)] = fine_kappa
    for d in range(2):
        halo_start(d, "kappa", 0)
    col_s[0] = fine_kappa[:, 0:2]
    col_s[1] = fine_kappa[:, QB - 2 : QB]
    for i, (dr, dc) in enumerate(DIRECTIONS[4:]):
        cor_s[i, 0] = fine_kappa[0 if dr < 0 else PB - 1, 0 if dc < 0 else QB - 1]
    for d in range(2, 8):
        halo_start(d, "kappa", 0)

    @pl.when(core == 0)
    def _():
        mine = pl.ds(0, 127)
        pltpu.make_async_remote_copy(
            src_ref=recv_c.at[mine], dst_ref=recv_c.at[mine], send_sem=crs_sem.at[0], recv_sem=crs_sem.at[1],
            device_id=me, device_id_type=LOGICAL,
        ).wait_recv()

    @pl.when(core == 1)
    def _():
        mine = pl.ds(0, 128)
        pltpu.make_async_remote_copy(
            src_ref=recv_c.at[mine], dst_ref=recv_c.at[mine], send_sem=crs_sem.at[0], recv_sem=crs_sem.at[1],
            device_id=me, device_id_type=LOGICAL,
        ).wait_recv()

    field_c = recv_c[...].reshape(128, LANES).T
    field_c = jnp.concatenate([field_c[:32], field_c[32:64]], axis=1)
    coarse_log = table_right(field_c, coarse_third)
    coarse_kappa = jnp.exp(coarse_log).reshape(PB // 2, QB // 2, N2 // 2)
    kc[pl.ds(2, PB // 2), pl.ds(EDGE, QB // 2)] = coarse_kappa
    ccol_s[0] = coarse_kappa[:, 0:2]
    ccol_s[1] = coarse_kappa[:, QB // 2 - 2 : QB // 2]
    for i, (dr, dc) in enumerate(DIRECTIONS[4:]):
        ccor_s[i, 0] = coarse_kappa[0 if dr < 0 else PB // 2 - 1, 0 if dc < 0 else QB // 2 - 1]
    for d in range(8):
        halo_start(d, "kappa", 1)

    def put_source(d, which):
        planes, width = (PB, QB) if which == 0 else (PB // 2, QB // 2)
        target, got = (fe, scol_r) if which == 0 else (fc, cscol_r)
        if d < 2:
            return None

        def store():
            at = EDGE - 1 if d == 2 else EDGE + width
            for plane in range(planes):
                target[1 + plane, pl.ds(at, 1)] = got[d - 2, plane]

        return store

    def put_kappa(d, which):
        planes, width = (PB, QB) if which == 0 else (PB // 2, QB // 2)
        target, cols, corners = (ke, col_r, cor_r) if which == 0 else (kc, ccol_r, ccor_r)
        if d < 2:
            return None

        def store():
            if d < 4:
                at = EDGE - 2 if d == 2 else EDGE + width
                for plane in range(planes):
                    target[2 + plane, pl.ds(at, 2)] = cols[d - 2, plane]
            else:
                dr, dc = DIRECTIONS[d]
                target[1 if dr < 0 else planes + 2, pl.ds(EDGE - 1 if dc < 0 else EDGE + width, 1)] = corners[d - 4]

        return store

    for d in range(4):
        for which in range(2):
            halo_wait(d, "source", which, put_source(d, which))
    for d in range(8):
        halo_wait(d, "kappa", 0, put_kappa(d, 0))
    smooth(ke, fe, ue, fine_out, PB, QB, N2)
    for d in range(8):
        halo_wait(d, "kappa", 1, put_kappa(d, 1))
    smooth(kc, fc, uc, coarse_out, PB // 2, QB // 2, N2 // 2)

    arrived.wait_send()
    back.wait_send()

    @pl.when(core == 0)
    def _():
        pltpu.make_async_remote_copy(
            src_ref=send_c.at[many], dst_ref=send_c.at[many], send_sem=crs_sem.at[0], recv_sem=crs_sem.at[1],
            device_id=me, device_id_type=LOGICAL,
        ).wait_send()


def body(noise, source):
    constants = tables()
    vmem, anywhere = pl.BlockSpec(memory_space=pltpu.VMEM), pl.BlockSpec(memory_space=pl.ANY)
    half_p, half_q, half_n = PB // 2, QB // 2, N2 // 2
    message = pltpu.VMEM((DEVICES, 2, LANES), F32)
    sems = pltpu.SemaphoreType.DMA
    return pl.pallas_call(
        kernel,
        out_shape=(
            jax.ShapeDtypeStruct((PB, QB, N2), F32),
            jax.ShapeDtypeStruct((half_p, half_q, half_n), F32),
        ),
        in_specs=[vmem, vmem] + [anywhere] * len(constants),
        out_specs=(vmem, vmem),
        scratch_shapes=[pltpu.VMEM(table.shape, table.dtype) for table in constants]
        + [message] * 4
        + [pltpu.VMEM((DEVICES, 1, LANES), F32), pltpu.VMEM((128, 1, LANES), F32)]
        + [
            pltpu.VMEM((PB + 4, QB + 16, N2), F32), pltpu.VMEM((PB + 2, QB + 16, N2), F32),
            pltpu.VMEM((PB + 2, QB + 16, N2), F32),
            pltpu.VMEM((half_p + 4, half_q + 16, half_n), F32), pltpu.VMEM((half_p + 2, half_q + 16, half_n), F32),
            pltpu.VMEM((half_p + 2, half_q + 16, half_n), F32),
        ]
        + [pltpu.VMEM((2, PB, 2, N2), F32)] * 2
        + [pltpu.VMEM((2, half_p, 2, half_n), F32)] * 2
        + [pltpu.VMEM((4, 1, N2), F32)] * 2
        + [pltpu.VMEM((4, 1, half_n), F32)] * 2
        + [pltpu.VMEM((2, PB, 1, N2), F32)] * 2
        + [pltpu.VMEM((2, half_p, 1, half_n), F32)] * 2
        + [sems((12,)), sems((2,)), sems((2,)), sems((2,)), sems]
        + [sems((8,))] * 4
        + [sems((4,))] * 4,
        compiler_params=pltpu.CompilerParams(collective_id=0, has_side_effects=True, vmem_limit_bytes=48 << 20),
    )(noise, source, *[jnp.asarray(table) for table in constants])


def solution(mesh):
    return jax.shard_map(
        body,
        mesh=mesh,
        in_specs=(P("row", ("level", "col"), None), P("row", ("level", "col"), None)),
        out_specs=(P("row", ("level", "col"), None), P("row", ("level", "col"), None)),
        check_vma=False,
    )
```

profile of v0, /device:TPU:1, one launch (start us, length us, event | category | flops | bytes accessed | tf_op | source)
XLA Modules:
  0.0 85.2 jit_solution(11580777725427204622)
XLA Ops:
  0.6 0.0 copy-start.13
  0.6 0.7 copy-done.13
  1.3 0.0 copy-start
  1.3 1.2 %copy-done = bf16[2,512,512]{2,1,0:T(8,128)(2,1)S(1)} copy-done((bf16[2,512,512]{2,1,0:T(8,128)(2,1)S(1)}, bf16[2,512,512]{2,1,0:T(8,128)(2,1)}, u32[]{:S(2)}) %copy-start) | copy-done | bytes 1048600
  2.6 0.0 copy-start.1
  2.6 1.2 %copy-done.1 = bf16[2,512,512]{2,1,0:T(8,128)(2,1)S(1)} copy-done((bf16[2,512,512]{2,1,0:T(8,128)(2,1)S(1)}, bf16[2,512,512]{2,1,0:T(8,128)(2,1)}, u32[]{:S(2)}) %copy-start.1) | copy-done | bytes 1048600
  3.8 0.0 copy-start.2
  3.8 1.2 %copy-done.2 = bf16[2,512,512]{2,1,0:T(8,128)(2,1)S(1)} copy-done((bf16[2,512,512]{2,1,0:T(8,128)(2,1)S(1)}, bf16[2,512,512]{2,1,0:T(8,128)(2,1)}, u32[]{:S(2)}) %copy-start.2) | copy-done | bytes 1048600
  5.0 0.0 copy-start.3
  5.0 1.0 %copy-done.3 = f32[3,256,128]{2,1,0:T(8,128)S(1)} copy-done((f32[3,256,128]{2,1,0:T(8,128)S(1)}, f32[3,256,128]{2,1,0:T(8,128)}, u32[]{:S(2)}) %copy-start.3) | copy-done | bytes 393240
  6.0 0.0 copy-start.4
  6.0 0.9 %copy-done.4 = f32[2,256,128]{2,1,0:T(8,128)S(1)} copy-done((f32[2,256,128]{2,1,0:T(8,128)S(1)}, f32[2,256,128]{2,1,0:T(8,128)}, u32[]{:S(2)}) %copy-start.4) | copy-done | bytes 262168
  7.0 0.0 copy-start.5
  7.0 0.9 %copy-done.5 = f32[2,256,128]{2,1,0:T(8,128)S(1)} copy-done((f32[2,256,128]{2,1,0:T(8,128)S(1)}, f32[2,256,128]{2,1,0:T(8,128)}, u32[]{:S(2)}) %copy-start.5) | copy-done | bytes 262168
  7.9 0.0 copy-start.6
  7.9 0.9 %copy-done.6 = bf16[512,256]{1,0:T(8,128)(2,1)S(1)} copy-done((bf16[512,256]{1,0:T(8,128)(2,1)S(1)}, bf16[512,256]{1,0:T(8,128)(2,1)}, u32[]{:S(2)}) %copy-start.6) | copy-done | bytes 262168
  8.9 0.0 copy-start.7
  8.9 0.9 %copy-done.7 = bf16[2,256,256]{2,1,0:T(8,128)(2,1)S(1)} copy-done((bf16[2,256,256]{2,1,0:T(8,128)(2,1)S(1)}, bf16[2,256,256]{2,1,0:T(8,128)(2,1)}, u32[]{:S(2)}) %copy-start.7) | copy-done | bytes 262168
  9.8 0.0 copy-start.8
  9.8 0.9 %copy-done.8 = bf16[2,256,256]{2,1,0:T(8,128)(2,1)S(1)} copy-done((bf16[2,256,256]{2,1,0:T(8,128)(2,1)S(1)}, bf16[2,256,256]{2,1,0:T(8,128)(2,1)}, u32[]{:S(2)}) %copy-start.8) | copy-done | bytes 262168
  10.8 0.0 copy-start.9
  10.8 0.9 %copy-done.9 = bf16[2,256,256]{2,1,0:T(8,128)(2,1)S(1)} copy-done((bf16[2,256,256]{2,1,0:T(8,128)(2,1)S(1)}, bf16[2,256,256]{2,1,0:T(8,128)(2,1)}, u32[]{:S(2)}) %copy-start.9) | copy-done | bytes 262168
  11.7 0.0 copy-start.10
  11.7 0.9 %copy-done.10 = bf16[2,256,256]{2,1,0:T(8,128)(2,1)S(1)} copy-done((bf16[2,256,256]{2,1,0:T(8,128)(2,1)S(1)}, bf16[2,256,256]{2,1,0:T(8,128)(2,1)}, u32[]{:S(2)}) %copy-start.10) | copy-done | bytes 262168
  12.7 0.0 copy-start.11
  12.7 0.9 %copy-done.11 = bf16[4,32,512]{2,1,0:T(8,128)(2,1)S(1)} copy-done((bf16[4,32,512]{2,1,0:T(8,128)(2,1)S(1)}, bf16[4,32,512]{2,1,0:T(8,128)(2,1)}, u32[]{:S(2)}) %copy-start.11) | copy-done | bytes 131096
  13.6 0.0 copy-start.12
  13.6 0.9 %copy-done.12 = bf16[4,32,512]{2,1,0:T(8,128)(2,1)S(1)} copy-done((bf16[4,32,512]{2,1,0:T(8,128)(2,1)S(1)}, bf16[4,32,512]{2,1,0:T(8,128)(2,1)}, u32[]{:S(2)}) %copy-start.12) | copy-done | bytes 131096
  14.5 69.4 %shard_map.149 = (f32[4,32,512]{2,1,0:T(8,128)S(1)}, f32[2,16,256]{2,1,0:T(8,128)S(1)}) custom-call(bf16[4,32,512]{2,1,0:T(8,128)(2,1)S(1)} %copy-done.11, bf16[4,32,512]{2,1,0:T(8,128)(2,1)S(1)} %copy-done.12, bf16[2,512,512]{2,1,0:T(8,128)(2,1)S(1)} %copy-done.2, bf16[2,512,512]{2,1,0:T(8,128)(2,1)S(1)} %copy-done.1, bf16[2,512,512]{2,1,0:T(8,128)(2,1)S(1)} %copy-done, ...), custom_call_target="tpu_custom_call" | custom-call | tf_op jit(solution)/shard_map/pallas_call | solution.py:480
  83.8 0.7 copy.18
  84.6 0.6 copy.19
Async XLA Ops:
  0.6 0.7 copy-start.13
  1.3 1.2 %copy-start = (bf16[2,512,512]{2,1,0:T(8,128)(2,1)S(1)}, bf16[2,512,512]{2,1,0:T(8,128)(2,1)}, u32[]{:S(2)}) copy-start(bf16[2,512,512]{2,1,0:T(8,128)(2,1)} %constant.26.clone.outer_t_h) | copy-start | bytes 3145732
  2.6 1.2 %copy-start.1 = (bf16[2,512,512]{2,1,0:T(8,128)(2,1)S(1)}, bf16[2,512,512]{2,1,0:T(8,128)(2,1)}, u32[]{:S(2)}) copy-start(bf16[2,512,512]{2,1,0:T(8,128)(2,1)} %constant.25.clone.outer_h) | copy-start | bytes 3145732
  3.8 1.2 %copy-start.2 = (bf16[2,512,512]{2,1,0:T(8,128)(2,1)S(1)}, bf16[2,512,512]{2,1,0:T(8,128)(2,1)}, u32[]{:S(2)}) copy-start(bf16[2,512,512]{2,1,0:T(8,128)(2,1)} %constant.24.clone.third_h) | copy-start | bytes 3145732
  5.0 1.0 %copy-start.3 = (f32[3,256,128]{2,1,0:T(8,128)S(1)}, f32[3,256,128]{2,1,0:T(8,128)}, u32[]{:S(2)}) copy-start(f32[3,256,128]{2,1,0:T(8,128)} %constant.35.clone.waves_h) | copy-start | bytes 1179652
  6.0 0.9 %copy-start.4 = (f32[2,256,128]{2,1,0:T(8,128)S(1)}, f32[2,256,128]{2,1,0:T(8,128)}, u32[]{:S(2)}) copy-start(f32[2,256,128]{2,1,0:T(8,128)} %constant.34.clone.twist_c_h) | copy-start | bytes 786436
  7.0 0.9 %copy-start.5 = (f32[2,256,128]{2,1,0:T(8,128)S(1)}, f32[2,256,128]{2,1,0:T(8,128)}, u32[]{:S(2)}) copy-start(f32[2,256,128]{2,1,0:T(8,128)} %constant.33.clone.twist_h) | copy-start | bytes 786436
  7.9 0.9 %copy-start.6 = (bf16[512,256]{1,0:T(8,128)(2,1)S(1)}, bf16[512,256]{1,0:T(8,128)(2,1)}, u32[]{:S(2)}) copy-start(bf16[512,256]{1,0:T(8,128)(2,1)} %constant.31.clone.pool_h) | copy-start | bytes 786436
  8.9 0.9 %copy-start.7 = (bf16[2,256,256]{2,1,0:T(8,128)(2,1)S(1)}, bf16[2,256,256]{2,1,0:T(8,128)(2,1)}, u32[]{:S(2)}) copy-start(bf16[2,256,256]{2,1,0:T(8,128)(2,1)} %constant.30.clone.coarse_third_h) | copy-start | bytes 786436
  9.8 0.9 %copy-start.8 = (bf16[2,256,256]{2,1,0:T(8,128)(2,1)S(1)}, bf16[2,256,256]{2,1,0:T(8,128)(2,1)}, u32[]{:S(2)}) copy-start(bf16[2,256,256]{2,1,0:T(8,128)(2,1)} %constant.29.clone.inner_c_h) | copy-start | bytes 786436
  10.8 0.9 %copy-start.9 = (bf16[2,256,256]{2,1,0:T(8,128)(2,1)S(1)}, bf16[2,256,256]{2,1,0:T(8,128)(2,1)}, u32[]{:S(2)}) copy-start(bf16[2,256,256]{2,1,0:T(8,128)(2,1)} %constant.28.clone.inner_t_h) | copy-start | bytes 786436
  11.7 0.9 %copy-start.10 = (bf16[2,256,256]{2,1,0:T(8,128)(2,1)S(1)}, bf16[2,256,256]{2,1,0:T(8,128)(2,1)}, u32[]{:S(2)}) copy-start(bf16[2,256,256]{2,1,0:T(8,128)(2,1)} %constant.27.clone.inner_h) | copy-start | bytes 786436
  12.7 0.9 %copy-start.11 = (bf16[4,32,512]{2,1,0:T(8,128)(2,1)S(1)}, bf16[4,32,512]{2,1,0:T(8,128)(2,1)}, u32[]{:S(2)}) copy-start(bf16[4,32,512]{2,1,0:T(8,128)(2,1)} %noise.1) | copy-start | bytes 393220
  13.6 0.9 %copy-start.12 = (bf16[4,32,512]{2,1,0:T(8,128)(2,1)S(1)}, bf16[4,32,512]{2,1,0:T(8,128)(2,1)}, u32[]{:S(2)}) copy-start(bf16[4,32,512]{2,1,0:T(8,128)(2,1)} %source.1) | copy-start | bytes 393220
where the time goes:
time: 85.7 us; the launch traced here: 85.2 us
  Pallas kernels  69.4 us (81%)
  local copies, waits for them, and re-layouts  15.1 us (18%)
    pallas_call x1, Pallas kernels, body(): pl.pallas_call(kernel, out_shape=(jax.ShapeDtypeStruct((PB, QB, N2), F32)...  69.4 us
    unnamed x30, local copies, waits for them, and re-layouts  15.1 us

commit v1 on v0

--- a/solution.py
+++ b/solution.py
@@ -188,11 +188,34 @@
 
     barrier = pltpu.get_barrier_semaphore()
 
-    def greet(i, carry):
-        pl.semaphore_signal(barrier, inc=1, device_id=(me + i) % DEVICES, device_id_type=LOGICAL)
-        return carry
-
-    lax.fori_loop(1, DEVICES, greet, 0, unroll=15)
+    columns = []
+    for k in reversed(range(COLS)):
+        y = lax.rem(col // 2 + k // 4, 4)
+        x = lax.rem((col % 2) * 2 + level + k % 4, 4)
+        x_hi, x_lo = x // 2, lax.rem(x, 2)
+        columns.append((x_lo * 8 + y * 2 + x_hi, x_lo * 128 + y * 2 + x_hi))
+
+    def row_at(i):
+        j = i // 2
+        half = (j + 1) // 2
+        z = lax.rem(row // 2 + 4 + (1 - 2 * lax.rem(j, 2)) * half, 8)
+        return z * 2 + lax.rem(core + 1 + i, 2)
+
+    def for_all_peers(step):
+        def one_row(i, carry):
+            r = row_at(i)
+            for c, part in columns:
+                step(r * COLS + c, r * 8 + part)
+            return carry
+
+        lax.fori_loop(0, ROWS - 1, one_row, 0)
+        for c, part in columns[:-1]:
+            step(row * COLS + c, row * 8 + part)
+
+    def greet(there, device):
+        pl.semaphore_signal(barrier, inc=1, device_id=device, device_id_type=LOGICAL)
+
+    for_all_peers(greet)
 
     pairs = (
         (third_h, third_t), (pool_h, pool), (pool_rows_h, pool_rows), (outer_h, outer), (twist_h, twist), (inner_h, inner), (waves_h, waves),
@@ -222,26 +245,13 @@
 
     pl.semaphore_wait(barrier, DEVICES - 1)
 
-    def peer_at(i):
-        j = i // 32
-        half = (j + 1) // 2
-        z = (row // 2 + 4 + jnp.where(j % 2 == 1, -half, half)) % 8
-        k = 31 - i % 32
-        r = z * 2 + (core + k // 16) % 2
-        y = (col // 2 + (k // 4) % 4) % 4
-        x = ((col % 2) * 2 + level + k % 4) % 4
-        c = (x % 2) * 8 + y * 2 + x // 2
-        return r, c
-
-    def push(i, carry):
-        r, c = peer_at(i)
+    def push(there, device):
         pltpu.make_async_remote_copy(
-            src_ref=send_f.at[r * COLS + c], dst_ref=recv_f.at[place], send_sem=fwd_sem.at[0], recv_sem=fwd_sem.at[1],
-            device_id=flat_id(r, c), device_id_type=LOGICAL,
+            src_ref=send_f.at[there], dst_ref=recv_f.at[place], send_sem=fwd_sem.at[0], recv_sem=fwd_sem.at[1],
+            device_id=device, device_id_type=LOGICAL,
         ).start()
-        return carry
-
-    lax.fori_loop(0, DEVICES - 1, push, 0, unroll=15)
+
+    for_all_peers(push)
     recv_f[place] = send_f[place]
 
     def neighbour(d):
@@ -350,29 +360,27 @@
     send_i[...] = planes[:, :LANES].reshape(DEVICES, 2, LANES)
     send_c[...] = planes[:, LANES:].reshape(DEVICES, 2, LANES)[:, 0:1, :]
 
-    def push_back(i, carry):
-        r, c = peer_at(i)
+    def push_back(there, device):
         pltpu.make_async_remote_copy(
-            src_ref=send_i.at[r * COLS + c], dst_ref=recv_i.at[place], send_sem=inv_sem.at[0], recv_sem=inv_sem.at[1],
-            device_id=flat_id(r, c), device_id_type=LOGICAL,
+            src_ref=send_i.at[there], dst_ref=recv_i.at[place], send_sem=inv_sem.at[0], recv_sem=inv_sem.at[1],
+            device_id=device, device_id_type=LOGICAL,
         ).start()
-        return carry
-
-    def push_coarse(i, carry):
-        r, c = peer_at(i)
+
+    coarse_place = (row // 2) * COLS + group
+
+    def push_coarse(there, device):
         pltpu.make_async_remote_copy(
-            src_ref=send_c.at[r * COLS + c], dst_ref=recv_c.at[(row // 2) * COLS + group], send_sem=crs_sem.at[0],
-            recv_sem=crs_sem.at[1], device_id=flat_id(r, c), device_id_type=LOGICAL,
+            src_ref=send_c.at[there], dst_ref=recv_c.at[coarse_place], send_sem=crs_sem.at[0],
+            recv_sem=crs_sem.at[1], device_id=device, device_id_type=LOGICAL,
         ).start()
-        return carry
-
-    lax.fori_loop(0, DEVICES - 1, push_back, 0, unroll=15)
+
+    for_all_peers(push_back)
     recv_i[place] = send_i[place]
 
     @pl.when(core == 0)
     def _():
-        lax.fori_loop(0, DEVICES - 1, push_coarse, 0, unroll=15)
-        recv_c[(row // 2) * COLS + group] = send_c[place]
+        for_all_peers(push_coarse)
+        recv_c[coarse_place] = send_c[place]
 
     back = pltpu.make_async_remote_copy(
         src_ref=send_i.at[many], dst_ref=recv_i.at[many], send_sem=inv_sem.at[0], recv_sem=inv_sem.at[1], device_id=me,
@@ -503,7 +511,7 @@
         + [sems((12,)), sems((2,)), sems((2,)), sems((2,)), sems]
         + [sems((8,))] * 4
         + [sems((4,))] * 4,
-        compiler_params=pltpu.CompilerParams(collective_id=0, has_side_effects=True, vmem_limit_bytes=48 << 20),
+        compiler_params=pltpu.CompilerParams(collective_id=0, has_side_effects=True, vmem_limit_bytes=60 << 20),
     )(noise, source, *[jnp.asarray(table) for table in constants])
 
 

time: 85.7 us -> 49 us (0.57)
  Pallas kernels: 69.4 us -> 45.9 us
  local copies, waits for them, and re-layouts: 15.1 us -> 2.3 us
    pallas_call x1, Pallas kernels: 69.4 us -> 45.9 us  [body(): pl.pallas_call(kernel, out_shape=(jax.ShapeDtypeStruct((PB, QB, N2), F32)...]
    unnamed x30 -> x4, local copies, waits for them, and re-layouts: 15.1 us -> 2.3 us
where the time goes in v1:
time: 49 us; the launch traced here: 48.9 us
  Pallas kernels  45.9 us (94%)
  local copies, waits for them, and re-layouts  2.3 us (5%)
  between operations  0.65 us (1%)
    pallas_call x1, Pallas kernels, body(): pl.pallas_call(kernel, out_shape=(jax.ShapeDtypeStruct((PB, QB, N2), F32)...  45.9 us
    unnamed x4, local copies, waits for them, and re-layouts  2.3 us

profile of v1, /device:TPU:1, one launch (start us, length us, event | category | flops | bytes accessed | tf_op | source)
XLA Modules:
  0.0 48.9 jit_solution(12824701541108185410)
XLA Ops:
  0.6 45.9 %shard_map.149 = (f32[4,32,512]{2,1,0:T(8,128)}, f32[2,16,256]{2,1,0:T(8,128)}) custom-call(bf16[4,32,512]{2,1,0:T(8,128)(2,1)} %noise.1, bf16[4,32,512]{2,1,0:T(8,128)(2,1)} %source.1, bf16[2,512,512]{2,1,0:T(8,128)(2,1)} %constant.24.clone.third_h, bf16[2,512,512]{2,1,0:T(8,128)(2,1)} %constant.25.clone.outer_h, ...), custom_call_target="tpu_custom_call" | custom-call | tf_op jit(solution)/shard_map/pallas_call | solution.py:488
  46.6 0.0 copy-start
  46.6 1.7 %copy.18 = f32[4,32,512]{2,1,0:T(8,128)} copy(f32[4,32,512]{2,1,0:T(8,128)} %get-tuple-element.4) | data formatting | bytes 524288
  48.3 0.0 copy-done
  48.3 0.6 %copy.19 = f32[2,16,256]{2,1,0:T(8,128)} copy(f32[2,16,256]{2,1,0:T(8,128)S(1)} %copy-done) | data formatting | bytes 65536
Async XLA Ops:
  46.6 1.7 %copy-start = (f32[2,16,256]{2,1,0:T(8,128)S(1)}, f32[2,16,256]{2,1,0:T(8,128)}, u32[]{:S(2)}) copy-start(f32[2,16,256]{2,1,0:T(8,128)} %get-tuple-element.5) | copy-start | bytes 98308

commit v2 on v1

v2 whole, which is shorter than its diff:
```python
import functools
import math

import jax
import jax.numpy as jnp
import ml_dtypes
import numpy as np
from jax import lax
from jax.experimental import pallas as pl
from jax.experimental.pallas import tpu as pltpu
from jax.sharding import PartitionSpec as P

JACOBI_WEIGHT = 2.0 / 3.0
CORRELATION = 0.2
FIELD_SCALE = 0.3
LOGICAL = pl.DeviceIdType.LOGICAL
F32 = jnp.float32
BF16 = jnp.bfloat16

N0, N1, N2 = 64, 512, 512
ROWS, COLS = 16, 16
DEVICES = ROWS * COLS
PB, QB = N0 // ROWS, N1 // COLS
LANES = PB * QB
CP, CQ = PB // 2 + 4, QB // 2 + 4
CELLS = CP * CQ
VMEM_LIMIT = 60 << 20
EDGE = 8


def split_table(table):
    high = table.astype(ml_dtypes.bfloat16)
    low = (table - high.astype(np.float64)).astype(ml_dtypes.bfloat16)
    return high, low


def signed(index, length):
    return np.where(index < length // 2, index, index - length).astype(np.float64)


def columns_of(column):
    y, x = column // 4, column % 4
    return (x % 2) * 8 + y * 2 + x // 2


@functools.lru_cache(maxsize=None)
def tables():
    place = np.arange(DEVICES)
    r, c = place % ROWS, columns_of(place // ROWS)
    third = (r % 2) * 128 + place // 2
    turn = 2.0 * np.pi
    n2 = np.arange(N2)
    angle = turn * ((third[:, None] * n2[None, :]) % N2) / N2
    third_table = np.stack([np.cos(angle), -np.sin(angle)], axis=1).reshape(2 * DEVICES, N2)
    k2 = np.arange(128)
    angle = turn * ((k2[:, None] * np.arange(N2 // 2)[None, :]) % (N2 // 2)) / (N2 // 2)
    coarse_third = np.stack([np.cos(angle), -np.sin(angle)], axis=1).reshape(256, N2 // 2)
    a, b = place // 16, place % 16
    angle = turn * ((a[:, None] * r[None, :] + b[:, None] * c[None, :]) % 16) / 16
    cos, sin = np.cos(angle), np.sin(angle)
    outer = np.concatenate([np.stack([cos, sin], axis=2), np.stack([-sin, cos], axis=2)], axis=0)
    outer = outer.reshape(2 * DEVICES, 2 * DEVICES)
    lane = np.arange(LANES)
    p, q = lane // QB, lane % QB
    angle = turn * (((8 * p[:, None] * p[None, :]) + q[:, None] * q[None, :]) % 32) / 32
    cos, sin = np.cos(angle), np.sin(angle)
    inner = np.block([[cos, -sin], [sin, cos]])
    lane_c = np.arange(CELLS)
    pc, qc = lane_c // CQ - 2, lane_c % CQ - 2
    angle = turn * (((8 * p[:, None] * pc[None, :]) + q[:, None] * qc[None, :]) % 16) / 16
    cos, sin = np.cos(angle), np.sin(angle)
    empty = np.zeros((LANES, LANES - CELLS))
    inner_c = np.block([[cos, empty, sin, empty], [-sin, empty, cos, empty]])
    angle = turn * ((8 * a[:, None] * p[None, :] + b[:, None] * q[None, :]) % 512) / 512
    twist = np.stack([np.cos(angle), np.sin(angle)])
    angle = turn * ((8 * a[:, None] * pc[None, :] + b[:, None] * qc[None, :]) % 256) / 256
    rest = np.zeros((DEVICES, LANES - CELLS))
    twist_c = np.stack([np.concatenate([np.cos(angle), rest], 1), np.concatenate([np.sin(angle), rest], 1)])
    m0 = signed(a[:, None] + 16 * p[None, :], N0)
    m1 = signed(b[:, None] + 16 * q[None, :], N1)
    norm = (float(N0) * N1 * N2) ** -0.5
    inside = (m0 != -N0 // 2) & (m1 != -N1 // 2)
    inside_c = (np.abs(m0) < N0 // 4) & (np.abs(m1) < N1 // 4)
    waves = np.stack([m0 * m0 + m1 * m1, inside * FIELD_SCALE * norm, inside_c * FIELD_SCALE * norm])
    pool = (np.arange(N2)[:, None] // 2 == np.arange(N2 // 2)[None, :]).astype(ml_dtypes.bfloat16)
    pool_rows = (np.arange(32)[:, None] == ((p // 2) * 16 + q // 2)[None, :]) * 0.125
    pool_rows = np.concatenate([pool_rows, np.zeros((32, LANES))], axis=1).astype(ml_dtypes.bfloat16)
    wide = np.concatenate([part for table in (third_table, outer, outer.T) for part in split_table(table)])
    narrow = np.concatenate([part for table in (inner, inner.T, inner_c, coarse_third) for part in split_table(table)])
    narrow = np.concatenate([narrow, pool, pool_rows])
    return wide, narrow, np.concatenate([twist, twist_c, waves]).astype(np.float32)


def halves(value):
    high = value.astype(BF16)
    return high, (value - high.astype(F32)).astype(BF16)


def dot(left, right):
    return jnp.dot(left, right, preferred_element_type=F32)


def table_left(table, value):
    high, low = halves(value)
    width = value.shape[1]
    both = dot(table[0], jnp.concatenate([high, low], axis=1))
    return both[:, :width] + (both[:, width:] + dot(table[1], high))


def table_right(value, table):
    high, low = halves(value)
    return dot(high, table[0]) + (dot(high, table[1]) + dot(low, table[0]))


DIRECTIONS = ((-1, 0), (1, 0), (0, -1), (0, 1), (-1, -1), (-1, 1), (1, -1), (1, 1))
OPPOSITE = (1, 0, 3, 2, 7, 6, 5, 4)


def flat_id(r, c):
    return (c // 8) * 128 + r * 8 + c % 8


def face_weight(center, beside):
    return jnp.where(beside > 0.0, 0.5 * (center + beside), center)


def smooth(kappa, source, first, out, planes, width, depth):
    tall = width + 2 * EDGE
    lane = lax.broadcasted_iota(jnp.int32, (tall, depth), 1)
    lane_in = lax.broadcasted_iota(jnp.int32, (width, depth), 1)
    diagonals = []
    for plane in range(planes + 2):
        center = kappa[plane + 1]
        diagonal = face_weight(center, kappa[plane + 2])
        diagonal = diagonal + face_weight(center, kappa[plane])
        diagonal = diagonal + face_weight(center, pltpu.roll(center, tall - 1, 0))
        diagonal = diagonal + face_weight(center, pltpu.roll(center, 1, 0))
        after = jnp.where(lane == depth - 1, 0.0, pltpu.roll(center, depth - 1, 1))
        before = jnp.where(lane == 0, 0.0, pltpu.roll(center, 1, 1))
        diagonal = diagonal + face_weight(center, after) + face_weight(center, before)
        guarded = jnp.where(center > 0.0, diagonal, 1.0)
        first[plane] = JACOBI_WEIGHT * source[plane] / guarded
    mid, low, high = pl.ds(EDGE, width), pl.ds(EDGE - 1, width), pl.ds(EDGE + 1, width)
    for plane in range(planes):
        center = kappa[plane + 2, mid]
        inner = first[plane + 1, mid]
        total = jnp.zeros_like(center)
        diagonal = jnp.zeros_like(center)
        for beside, value in (
            (kappa[plane + 3, mid], first[plane + 2, mid]),
            (kappa[plane + 1, mid], first[plane, mid]),
            (kappa[plane + 2, high], first[plane + 1, high]),
            (kappa[plane + 2, low], first[plane + 1, low]),
        ):
            face = face_weight(center, beside)
            diagonal = diagonal + face
            total = total + face * value
        for shift, missing in ((depth - 1, depth - 1), (1, 0)):
            outside = lane_in == missing
            beside = jnp.where(outside, 0.0, pltpu.roll(center, shift, 1))
            value = jnp.where(outside, 0.0, pltpu.roll(inner, shift, 1))
            face = face_weight(center, beside)
            diagonal = diagonal + face
            total = total + face * value
        residual = source[plane + 1, mid] - diagonal * inner + total
        out[plane] = inner + JACOBI_WEIGHT * residual / diagonal


def kernel(
    noise_h, source_h, wide_h, narrow_h, tables_h, fine_out, coarse_out,
    noise, source, wide, narrow, tables_v,
    send_f, recv_f, send_i, recv_i, send_c, recv_c,
    ke, fe, ue, kc, fc, uc,
    col_s, col_r, cor_s, cor_r, scol_s, scol_r, cscol_s, cscol_r,
    table_sem, fwd_sem, inv_sem, crs_sem, halo_s, halo_r, src_s, src_r, csrc_s, csrc_r,
):
    level, row, col = lax.axis_index("level"), lax.axis_index("row"), lax.axis_index("col")
    group = level * 8 + col
    me = flat_id(row, group)
    core, my_z = lax.rem(row, 2), row // 2
    my_y, my_x = col // 2, lax.rem(col, 2) * 2 + level
    place = (my_y * 4 + my_x) * ROWS + row
    half_p, half_q, half_n = PB // 2, QB // 2, N2 // 2

    rows = []
    for step in (4, 3, 5, 2, 6, 1, 7, 0):
        z2 = lax.rem(my_z + step, 8) * 2
        rows += [z2 + 1 - core, z2 + core]
    rows = [(r, r * 8) for r in rows]

    def far(i):
        return 2 + (1 - 2 * lax.rem(i, 2)) * ((i + 1) // 2)

    def for_column(i, j, step, count=ROWS):
        y, x = lax.rem(my_y + far(i), 4), lax.rem(my_x + far(j), 4)
        first, part = (y * 4 + x) * ROWS, lax.rem(x, 2) * 128 + y * 2 + x // 2
        for r, r8 in rows[:count]:
            step(first + r, part + r8)

    def for_all_peers(step):
        def one(i, carry):
            for_column(i // 4, lax.rem(i, 4), step)
            return carry

        lax.fori_loop(0, COLS - 1, one, 0)
        for_column(3, 3, step, ROWS - 1)

    barrier = pltpu.get_barrier_semaphore()

    def greet(there, device):
        pl.semaphore_signal(barrier, inc=1, device_id=device, device_id_type=LOGICAL)

    for ref in (ke, fe, fc):
        ref[...] = jnp.zeros_like(ref)

    for_all_peers(greet)

    size = 2 * DEVICES
    pairs = (
        (noise_h, noise), (source_h, source),
        (wide_h.at[pl.ds(0, 2 * size)], wide.at[pl.ds(0, 2 * size)]),
        (narrow_h, narrow), (tables_h, tables_v),
        (wide_h.at[pl.ds(2 * size, 4 * size)], wide.at[pl.ds(2 * size, 4 * size)]),
    )
    loads = [pltpu.make_async_copy(a, b, table_sem.at[i]) for i, (a, b) in enumerate(pairs)]
    for load in loads:
        load.start()

    class Parts:
        def __init__(self, ref, at, count):
            self.ref, self.at, self.count = ref, at, count

        def __getitem__(self, part):
            return self.ref[pl.ds(self.at + part * self.count, self.count)]

    third_t, outer, outer_t = (Parts(wide, i * 2 * size, size) for i in range(3))
    inner, inner_t, inner_c, coarse_third = (Parts(narrow, i * size, DEVICES) for i in range(4))
    twist, twist_c, waves = (tables_v.at[0], tables_v.at[1]), (tables_v.at[2], tables_v.at[3]), tables_v.at[pl.ds(4, 3)]

    loads[0].wait()
    loads[1].wait()
    loads[2].wait()
    noise_rows = noise[...].reshape(LANES, N2)
    contract = (((1,), (1,)), ((), ()))
    spectrum = lax.dot_general(third_t[0], noise_rows, contract, preferred_element_type=F32)
    spectrum = spectrum + lax.dot_general(third_t[1], noise_rows, contract, preferred_element_type=F32)
    send_f[...] = spectrum.reshape(DEVICES, 2, LANES)

    fe[pl.ds(1, PB), pl.ds(EDGE, QB)] = source[...].astype(F32)
    scol_s[0, :, 0] = source[:, 0].astype(F32)
    scol_s[1, :, 0] = source[:, QB - 1].astype(F32)

    pl.semaphore_wait(barrier, DEVICES - 1)

    def push(there, device):
        pltpu.make_async_remote_copy(
            src_ref=send_f.at[there], dst_ref=recv_f.at[place], send_sem=fwd_sem.at[0], recv_sem=fwd_sem.at[1],
            device_id=device, device_id_type=LOGICAL,
        ).start()

    for_all_peers(push)
    recv_f[place] = send_f[place]

    loads[3].wait()
    loads[4].wait()
    high, low = halves(dot(narrow[pl.ds(5 * size, 32), pl.ds(0, LANES)], source[...].reshape(LANES, N2)))
    pool = narrow[pl.ds(4 * size, size)]
    pooled = (dot(high, pool) + dot(low, pool)).reshape(half_p, half_q, half_n)
    fc[pl.ds(1, half_p), pl.ds(EDGE, half_q)] = pooled
    cscol_s[0, :, 0] = pooled[:, 0]
    cscol_s[1, :, 0] = pooled[:, half_q - 1]

    def neighbour(d):
        dr, dc = DIRECTIONS[d]
        r, c = row + dr, group + dc
        exists = (r >= 0) & (r < ROWS) & (c >= 0) & (c < COLS)
        return exists, flat_id(r, c)

    mid, mid_c = pl.ds(EDGE, QB), pl.ds(EDGE, half_q)

    def halo_copy(d, kind):
        back = OPPOSITE[d]
        if kind == "source":
            if d < 2:
                return (
                    fe.at[1 if d == 0 else PB, mid], fe.at[PB + 1 if d == 0 else 0, mid],
                    fe.at[0 if d == 0 else PB + 1, mid], src_s, src_r,
                )
            return scol_s.at[d - 2], scol_r.at[back - 2], scol_r.at[d - 2], src_s, src_r
        if kind == "coarse":
            if d < 2:
                return (
                    fc.at[1 if d == 0 else half_p, mid_c], fc.at[half_p + 1 if d == 0 else 0, mid_c],
                    fc.at[0 if d == 0 else half_p + 1, mid_c], csrc_s, csrc_r,
                )
            return cscol_s.at[d - 2], cscol_r.at[back - 2], cscol_r.at[d - 2], csrc_s, csrc_r
        if d < 2:
            return (
                ke.at[pl.ds(2 if d == 0 else PB, 2), mid], ke.at[pl.ds(PB + 2 if d == 0 else 0, 2), mid],
                ke.at[pl.ds(0 if d == 0 else PB + 2, 2), mid], halo_s, halo_r,
            )
        if d < 4:
            return col_s.at[d - 2], col_r.at[back - 2], col_r.at[d - 2], halo_s, halo_r
        return cor_s.at[d - 4], cor_r.at[back - 4], cor_r.at[d - 4], halo_s, halo_r

    def halo_start(d, kind):
        exists, there = neighbour(d)
        src, dst, _, s_sem, r_sem = halo_copy(d, kind)

        @pl.when(exists)
        def _():
            pltpu.make_async_remote_copy(
                src_ref=src, dst_ref=dst, send_sem=s_sem.at[d], recv_sem=r_sem.at[OPPOSITE[d]], device_id=there,
                device_id_type=LOGICAL,
            ).start()

    def halo_wait(d, kind, then):
        exists, there = neighbour(d)
        src, _, here, s_sem, r_sem = halo_copy(d, kind)

        @pl.when(exists)
        def _():
            copy = pltpu.make_async_remote_copy(
                src_ref=src, dst_ref=here, send_sem=s_sem.at[d], recv_sem=r_sem.at[d], device_id=there,
                device_id_type=LOGICAL,
            )
            copy.wait_send()
            copy.wait_recv()
            then(d)

    for d in range(4):
        halo_start(d, "source")
        halo_start(d, "coarse")

    third = core * 128 + place // 2
    third_f = third.astype(F32)
    weight = jnp.where(third == 0, 1.0, 2.0)
    damp = weight / (1.0 + (2.0 * math.pi * CORRELATION) ** 2 * (waves[0] + third_f * third_f))
    amp = waves[1] * damp
    amp_c = waves[2] * damp
    loads[5].wait()

    many = pl.ds(0, DEVICES - 1)
    arrived = pltpu.make_async_remote_copy(
        src_ref=send_f.at[many], dst_ref=recv_f.at[many], send_sem=fwd_sem.at[0], recv_sem=fwd_sem.at[1], device_id=me,
        device_id_type=LOGICAL,
    )
    arrived.wait_recv()

    z = table_left(outer, recv_f[...].reshape(size, LANES))
    z_re, z_im = z[:DEVICES], z[DEVICES:]
    cos, sin = twist[0][...], twist[1][...]
    turned = jnp.concatenate([z_re * cos + z_im * sin, z_im * cos - z_re * sin], axis=1)
    y = table_right(turned, inner)
    x = table_right(y * jnp.concatenate([amp, amp], axis=1), inner_t)
    x_re, x_im = x[:, :LANES], x[:, LANES:]
    xc = table_right(y * jnp.concatenate([amp_c, amp_c], axis=1), inner_c)
    xc_re, xc_im = xc[:, :LANES], xc[:, LANES:]
    cos_c, sin_c = twist_c[0][...], twist_c[1][...]
    fine_part = jnp.concatenate([x_re * cos - x_im * sin, x_im * cos + x_re * sin], axis=0)
    coarse_part = jnp.concatenate([xc_re * cos_c - xc_im * sin_c, xc_im * cos_c + xc_re * sin_c], axis=0)
    high, low = halves(jnp.concatenate([fine_part, coarse_part], axis=1))

    def push_back(there, device):
        pltpu.make_async_remote_copy(
            src_ref=send_i.at[there], dst_ref=recv_i.at[place], send_sem=inv_sem.at[0], recv_sem=inv_sem.at[1],
            device_id=device, device_id_type=LOGICAL,
        ).start()

    coarse_place = place // 2

    def push_coarse(there, device):
        pltpu.make_async_remote_copy(
            src_ref=send_c.at[there], dst_ref=recv_c.at[coarse_place], send_sem=crs_sem.at[0],
            recv_sem=crs_sem.at[1], device_id=device, device_id_type=LOGICAL,
        ).start()

    for i in range(4):
        y4 = lax.rem(my_y + (2, 1, 3, 0)[i], 4)
        upper = wide[pl.ds(4 * size + y4 * LANES, LANES)]
        lower = wide[pl.ds(5 * size + y4 * LANES, LANES)]
        planes = dot(upper, high) + (dot(upper, low) + dot(lower, high))
        send_i[pl.ds(y4 * 64, 64)] = planes[:, :LANES].reshape(64, 2, LANES)
        send_c[pl.ds(y4 * 64, 64)] = planes[:, LANES:].reshape(64, 2, LANES)

        def one(j, carry, i=i):
            for_column(i, j, push_back)
            return carry

        if i < 3:
            lax.fori_loop(0, 4, one, 0)
        else:
            lax.fori_loop(0, 3, one, 0)
            for_column(3, 3, push_back, ROWS - 1)
    recv_i[place] = send_i[place]

    @pl.when(core == 0)
    def _():
        for_all_peers(push_coarse)
        recv_c[coarse_place] = send_c[place]

    def put_source(d):
        if d >= 2:
            at = EDGE - 1 if d == 2 else EDGE + QB
            for plane in range(PB):
                fe[1 + plane, pl.ds(at, 1)] = scol_r[d - 2, plane]

    def put_coarse(d):
        if d >= 2:
            at = EDGE - 1 if d == 2 else EDGE + half_q
            for plane in range(half_p):
                fc[1 + plane, pl.ds(at, 1)] = cscol_r[d - 2, plane]

    def put_kappa(d):
        dr, dc = DIRECTIONS[d]
        if d >= 4:
            ke[1 if dr < 0 else PB + 2, pl.ds(EDGE - 1 if dc < 0 else EDGE + QB, 1)] = cor_r[d - 4]
        elif d >= 2:
            at = EDGE - 2 if d == 2 else EDGE + QB
            for plane in range(PB):
                ke[2 + plane, pl.ds(at, 2)] = col_r[d - 2, plane]

    for d in range(4):
        halo_wait(d, "source", put_source)
        halo_wait(d, "coarse", put_coarse)
    kc[...] = jnp.zeros_like(kc)
    arrived.wait_send()

    returned = pltpu.make_async_remote_copy(
        src_ref=send_i.at[many], dst_ref=recv_i.at[many], send_sem=inv_sem.at[0], recv_sem=inv_sem.at[1], device_id=me,
        device_id_type=LOGICAL,
    )
    returned.wait_recv()
    fine_log = table_right(recv_i[...].reshape(size, LANES).T, third_t)
    fine_kappa = jnp.exp(fine_log).reshape(PB, QB, N2)
    for i, (dr, dc) in enumerate(DIRECTIONS[4:]):
        cor_s[i, 0] = fine_kappa[0 if dr < 0 else PB - 1, 0 if dc < 0 else QB - 1]
    col_s[0] = fine_kappa[:, 0:2]
    col_s[1] = fine_kappa[:, QB - 2 : QB]
    ke[pl.ds(2, PB), mid] = fine_kappa
    for d in (4, 5, 6, 7, 2, 3, 0, 1):
        halo_start(d, "kappa")

    for own in range(2):

        @pl.when(core == own)
        def _(own=own):
            some = pl.ds(0, 127 + own)
            pltpu.make_async_remote_copy(
                src_ref=recv_c.at[some], dst_ref=recv_c.at[some], send_sem=crs_sem.at[0], recv_sem=crs_sem.at[1],
                device_id=me, device_id_type=LOGICAL,
            ).wait_recv()

    coarse_log = table_right(recv_c[...].reshape(DEVICES, LANES).T, coarse_third)
    cell = lax.broadcasted_iota(jnp.int32, (LANES, half_n), 0)
    n0 = row * half_p + lax.div(cell, CQ) - 2
    n1 = group * half_q + lax.rem(cell, CQ) - 2
    inside = (n0 >= 0) & (n0 < N0 // 2) & (n1 >= 0) & (n1 < N1 // 2)
    coarse_kappa = jnp.where(inside, jnp.exp(coarse_log), 0.0)
    for plane in range(CP):
        kc[plane, pl.ds(EDGE - 2, CQ)] = coarse_kappa[plane * CQ : (plane + 1) * CQ]
    smooth(kc, fc, uc, coarse_out, half_p, half_q, half_n)

    for d in (0, 1, 2, 3, 4, 5, 6, 7):
        halo_wait(d, "kappa", put_kappa)
    smooth(ke, fe, ue, fine_out, PB, QB, N2)

    returned.wait_send()

    @pl.when(core == 0)
    def _():
        pltpu.make_async_remote_copy(
            src_ref=send_c.at[many], dst_ref=send_c.at[many], send_sem=crs_sem.at[0], recv_sem=crs_sem.at[1],
            device_id=me, device_id_type=LOGICAL,
        ).wait_send()


def hand_over(fine, coarse, fine_out, coarse_out):
    fine_out[...] = fine[...]
    coarse_out[...] = coarse[...]


def body(noise, source):
    constants = tables()
    vmem, anywhere = pl.BlockSpec(memory_space=pltpu.VMEM), pl.BlockSpec(memory_space=pl.ANY)
    half_p, half_q, half_n = PB // 2, QB // 2, N2 // 2
    message = pltpu.VMEM((DEVICES, 2, LANES), F32)
    sems = pltpu.SemaphoreType.DMA
    pressures = pl.pallas_call(
        kernel,
        out_shape=(
            jax.ShapeDtypeStruct((PB, QB, N2), F32),
            jax.ShapeDtypeStruct((half_p, half_q, half_n), F32),
        ),
        in_specs=[anywhere] * 5,
        out_specs=(vmem, vmem),
        scratch_shapes=[pltpu.VMEM((PB, QB, N2), BF16)] * 2
        + [pltpu.VMEM(table.shape, table.dtype) for table in constants]
        + [message] * 5
        + [pltpu.VMEM((128, 2, LANES), F32)]
        + [
            pltpu.VMEM((PB + 4, QB + 16, N2), F32), pltpu.VMEM((PB + 2, QB + 16, N2), F32),
            pltpu.VMEM((PB + 2, QB + 16, N2), F32),
            pltpu.VMEM((half_p + 4, half_q + 16, half_n), F32), pltpu.VMEM((half_p + 2, half_q + 16, half_n), F32),
            pltpu.VMEM((half_p + 2, half_q + 16, half_n), F32),
        ]
        + [pltpu.VMEM((2, PB, 2, N2), F32)] * 2
        + [pltpu.VMEM((4, 1, N2), F32)] * 2
        + [pltpu.VMEM((2, PB, 1, N2), F32)] * 2
        + [pltpu.VMEM((2, half_p, 1, half_n), F32)] * 2
        + [sems((6,)), sems((2,)), sems((2,)), sems((2,))]
        + [sems((8,))] * 2
        + [sems((4,))] * 4,
        compiler_params=pltpu.CompilerParams(collective_id=0, has_side_effects=True, vmem_limit_bytes=VMEM_LIMIT),
    )(noise, source, *[jnp.asarray(table) for table in constants])
    return pl.pallas_call(
        hand_over,
        out_shape=tuple(jax.ShapeDtypeStruct(value.shape, value.dtype) for value in pressures),
        in_specs=[vmem] * 2,
        out_specs=(vmem, vmem),
    )(*pressures)


def solution(mesh):
    return jax.shard_map(
        body,
        mesh=mesh,
        in_specs=(P("row", ("level", "col"), None), P("row", ("level", "col"), None)),
        out_specs=(P("row", ("level", "col"), None), P("row", ("level", "col"), None)),
        check_vma=False,
    )
```

time: 49 us -> 45.1 us (0.920)
  local copies, waits for them, and re-layouts: 2.3 us -> 0 us
  Pallas kernels: 45.9 us -> 44.4 us
    pallas_call x1, Pallas kernels: 45.9 us -> 42.7 us  [body(): pl.pallas_call(kernel, out_shape=(jax.ShapeDtypeStruct((PB, QB, N2), F32)...]
    unnamed x4 -> x0, local copies, waits for them, and re-layouts: 2.3 us -> none
    pallas_call x0 -> x1, Pallas kernels: none -> 1.68 us  [body(): pl.pallas_call(hand_over, out_shape=tuple((jax.ShapeDtypeStruct(value.sha...]
where the time goes in v2:
time: 45.1 us; the launch traced here: 45 us
  Pallas kernels  44.4 us (98%)
  between operations  0.64 us (1%)
    pallas_call x1, Pallas kernels, body(): pl.pallas_call(kernel, out_shape=(jax.ShapeDtypeStruct((PB, QB, N2), F32)...  42.7 us
    pallas_call x1, Pallas kernels, body(): pl.pallas_call(hand_over, out_shape=tuple((jax.ShapeDtypeStruct(value.sha...  1.68 us

profile of v2, /device:TPU:1, one launch (start us, length us, event | category | flops | bytes accessed | tf_op | source)
XLA Modules:
  0.0 45.0 jit_solution(18254782383622848888)
XLA Ops:
  0.6 42.7 %shard_map.68 = (f32[4,32,512]{2,1,0:T(8,128)}, f32[2,16,256]{2,1,0:T(8,128)}) custom-call(bf16[4,32,512]{2,1,0:T(8,128)(2,1)} %noise_h.1, bf16[4,32,512]{2,1,0:T(8,128)(2,1)} %source_h.1, bf16[3072,512]{1,0:T(8,128)(2,1)} %constant.6.clone.wide_h, bf16[2592,256]{1,0:T(8,128)(2,1)} %constant.7.clone.narrow_h, f32[7,256,128]{2,1,0:T(8,128)} %constant.8.clone.tables_h), custom_call_target="tpu_custom_call" | custom-call | tf_op jit(solution)/shard_map/pallas_call | solution.py:489
  43.3 1.7 %shard_map.69 = (f32[4,32,512]{2,1,0:T(8,128)}, f32[2,16,256]{2,1,0:T(8,128)}) custom-call(f32[4,32,512]{2,1,0:T(8,128)} %get-tuple-element.4.fine, f32[2,16,256]{2,1,0:T(8,128)} %get-tuple-element.5.coarse), custom_call_target="tpu_custom_call" | custom-call | tf_op jit(solution)/shard_map/pallas_call | solution.py:516

commit v3 on v2

--- a/solution.py
+++ b/solution.py
@@ -25,6 +25,7 @@
 CP, CQ = PB // 2 + 4, QB // 2 + 4
 CELLS = CP * CQ
 VMEM_LIMIT = 60 << 20
+FAR = (2, 1, 3, 0)
 EDGE = 8
 
 
@@ -100,13 +101,6 @@
     return jnp.dot(left, right, preferred_element_type=F32)
 
 
-def table_left(table, value):
-    high, low = halves(value)
-    width = value.shape[1]
-    both = dot(table[0], jnp.concatenate([high, low], axis=1))
-    return both[:, :width] + (both[:, width:] + dot(table[1], high))
-
-
 def table_right(value, table):
     high, low = halves(value)
     return dot(high, table[0]) + (dot(high, table[1]) + dot(low, table[0]))
@@ -124,41 +118,52 @@
     return jnp.where(beside > 0.0, 0.5 * (center + beside), center)
 
 
-def smooth(kappa, source, first, out, planes, width, depth):
-    tall = width + 2 * EDGE
-    lane = lax.broadcasted_iota(jnp.int32, (tall, depth), 1)
-    lane_in = lax.broadcasted_iota(jnp.int32, (width, depth), 1)
-    diagonals = []
+def beside_lanes(value, missing):
+    depth = value.shape[-1]
+    lane = lax.broadcasted_iota(jnp.int32, value.shape, 1)
+    after = jnp.where(lane == depth - 1, missing, pltpu.roll(value, depth - 1, 1))
+    before = jnp.where(lane == 0, missing, pltpu.roll(value, 1, 1))
+    return after, before
+
+
+def first_sweep(center, neighbours, source):
+    diagonal = face_weight(center, neighbours[0])
+    for beside in neighbours[1:]:
+        diagonal = diagonal + face_weight(center, beside)
+    return JACOBI_WEIGHT * source / jnp.where(center > 0.0, diagonal, 1.0)
+
+
+def smooth(kappa, source, first, out, planes, width):
+    mid, low, high = pl.ds(EDGE, width), pl.ds(EDGE - 1, width), pl.ds(EDGE + 1, width)
     for plane in range(planes + 2):
-        center = kappa[plane + 1]
-        diagonal = face_weight(center, kappa[plane + 2])
-        diagonal = diagonal + face_weight(center, kappa[plane])
-        diagonal = diagonal + face_weight(center, pltpu.roll(center, tall - 1, 0))
-        diagonal = diagonal + face_weight(center, pltpu.roll(center, 1, 0))
-        after = jnp.where(lane == depth - 1, 0.0, pltpu.roll(center, depth - 1, 1))
-        before = jnp.where(lane == 0, 0.0, pltpu.roll(center, 1, 1))
-        diagonal = diagonal + face_weight(center, after) + face_weight(center, before)
-        guarded = jnp.where(center > 0.0, diagonal, 1.0)
-        first[plane] = JACOBI_WEIGHT * source[plane] / guarded
-    mid, low, high = pl.ds(EDGE, width), pl.ds(EDGE - 1, width), pl.ds(EDGE + 1, width)
+        center = kappa[plane + 1, mid]
+        near = (kappa[plane + 2, mid], kappa[plane, mid], kappa[plane + 1, high], kappa[plane + 1, low])
+        first[plane, mid] = first_sweep(center, near + beside_lanes(center, 0.0), source[plane, mid])
+    for at, inward, outward in ((EDGE - 1, EDGE, EDGE - 2), (EDGE + width, EDGE + width - 1, EDGE + width + 1)):
+
+        def line(ref, base, q):
+            return jnp.concatenate([ref[base + plane, pl.ds(q, 1)] for plane in range(planes)], axis=0)
+
+        center = line(kappa, 2, at)
+        near = (line(kappa, 3, at), line(kappa, 1, at), line(kappa, 2, inward), line(kappa, 2, outward))
+        value = first_sweep(center, near + beside_lanes(center, 0.0), line(source, 1, at))
+        for plane in range(planes):
+            first[1 + plane, pl.ds(at, 1)] = value[plane : plane + 1]
     for plane in range(planes):
         center = kappa[plane + 2, mid]
         inner = first[plane + 1, mid]
         total = jnp.zeros_like(center)
         diagonal = jnp.zeros_like(center)
+        after, before = beside_lanes(center, 0.0)
+        after_value, before_value = beside_lanes(inner, 0.0)
         for beside, value in (
             (kappa[plane + 3, mid], first[plane + 2, mid]),
             (kappa[plane + 1, mid], first[plane, mid]),
             (kappa[plane + 2, high], first[plane + 1, high]),
             (kappa[plane + 2, low], first[plane + 1, low]),
+            (after, after_value),
+            (before, before_value),
         ):
-            face = face_weight(center, beside)
-            diagonal = diagonal + face
-            total = total + face * value
-        for shift, missing in ((depth - 1, depth - 1), (1, 0)):
-            outside = lane_in == missing
-            beside = jnp.where(outside, 0.0, pltpu.roll(center, shift, 1))
-            value = jnp.where(outside, 0.0, pltpu.roll(inner, shift, 1))
             face = face_weight(center, beside)
             diagonal = diagonal + face
             total = total + face * value
@@ -172,7 +177,7 @@
     send_f, recv_f, send_i, recv_i, send_c, recv_c,
     ke, fe, ue, kc, fc, uc,
     col_s, col_r, cor_s, cor_r, scol_s, scol_r, cscol_s, cscol_r,
-    table_sem, fwd_sem, inv_sem, crs_sem, halo_s, halo_r, src_s, src_r, csrc_s, csrc_r,
+    table_sem, fwd_s, fwd_r, inv_s, inv_r, crs_sem, halo_s, halo_r, src_s, src_r, csrc_s, csrc_r,
 ):
     level, row, col = lax.axis_index("level"), lax.axis_index("row"), lax.axis_index("col")
     group = level * 8 + col
@@ -188,30 +193,34 @@
         rows += [z2 + 1 - core, z2 + core]
     rows = [(r, r * 8) for r in rows]
 
-    def far(i):
-        return 2 + (1 - 2 * lax.rem(i, 2)) * ((i + 1) // 2)
+    def far(j):
+        return 2 + (1 - 2 * lax.rem(j, 2)) * ((j + 1) // 2)
 
     def for_column(i, j, step, count=ROWS):
-        y, x = lax.rem(my_y + far(i), 4), lax.rem(my_x + far(j), 4)
+        y, x = lax.rem(my_y + FAR[i], 4), lax.rem(my_x + far(j), 4)
         first, part = (y * 4 + x) * ROWS, lax.rem(x, 2) * 128 + y * 2 + x // 2
         for r, r8 in rows[:count]:
-            step(first + r, part + r8)
+            step(i, first + r, part + r8)
+
+    def for_quarter(i, step):
+        def one(j, carry):
+            for_column(i, j, step)
+            return carry
+
+        if i < 3:
+            lax.fori_loop(0, 4, one, 0)
+        else:
+            lax.fori_loop(0, 3, one, 0)
+            for_column(3, 3, step, ROWS - 1)
 
     def for_all_peers(step):
-        def one(i, carry):
-            for_column(i // 4, lax.rem(i, 4), step)
-            return carry
-
-        lax.fori_loop(0, COLS - 1, one, 0)
-        for_column(3, 3, step, ROWS - 1)
+        for i in range(4):
+            for_quarter(i, step)
 
     barrier = pltpu.get_barrier_semaphore()
 
-    def greet(there, device):
+    def greet(i, there, device):
         pl.semaphore_signal(barrier, inc=1, device_id=device, device_id_type=LOGICAL)
-
-    for ref in (ke, fe, fc):
-        ref[...] = jnp.zeros_like(ref)
 
     for_all_peers(greet)
 
@@ -233,9 +242,21 @@
         def __getitem__(self, part):
             return self.ref[pl.ds(self.at + part * self.count, self.count)]
 
-    third_t, outer, outer_t = (Parts(wide, i * 2 * size, size) for i in range(3))
+    third_t = Parts(wide, 0, size)
     inner, inner_t, inner_c, coarse_third = (Parts(narrow, i * size, DEVICES) for i in range(4))
     twist, twist_c, waves = (tables_v.at[0], tables_v.at[1]), (tables_v.at[2], tables_v.at[3]), tables_v.at[pl.ds(4, 3)]
+
+    for ref, width in ((ke, QB), (fe, QB), (fc, half_q)):
+        for at in (0, EDGE + width):
+            ref[:, pl.ds(at, EDGE)] = jnp.zeros((ref.shape[0], EDGE, ref.shape[2]), F32)
+
+    for edge, last in ((0, False), (ROWS - 1, True)):
+
+        @pl.when(row == edge)
+        def _(last=last):
+            for ref, width, layers in ((ke, QB, 2), (fe, QB, 1), (fc, half_q, 1)):
+                at = ref.shape[0] - layers if last else 0
+                ref[pl.ds(at, layers), pl.ds(EDGE, width)] = jnp.zeros((layers, width, ref.shape[2]), F32)
 
     loads[0].wait()
     loads[1].wait()
@@ -252,9 +273,9 @@
 
     pl.semaphore_wait(barrier, DEVICES - 1)
 
-    def push(there, device):
+    def push(i, there, device):
         pltpu.make_async_remote_copy(
-            src_ref=send_f.at[there], dst_ref=recv_f.at[place], send_sem=fwd_sem.at[0], recv_sem=fwd_sem.at[1],
+            src_ref=send_f.at[there], dst_ref=recv_f.at[place], send_sem=fwd_s, recv_sem=fwd_r.at[i],
             device_id=device, device_id_type=LOGICAL,
         ).start()
 
@@ -340,14 +361,22 @@
     amp_c = waves[2] * damp
     loads[5].wait()
 
-    many = pl.ds(0, DEVICES - 1)
-    arrived = pltpu.make_async_remote_copy(
-        src_ref=send_f.at[many], dst_ref=recv_f.at[many], send_sem=fwd_sem.at[0], recv_sem=fwd_sem.at[1], device_id=me,
-        device_id_type=LOGICAL,
-    )
-    arrived.wait_recv()
-
-    z = table_left(outer, recv_f[...].reshape(size, LANES))
+    def copies_of(send, got, s_sem, r_sem, count):
+        some = pl.ds(0, count)
+        return pltpu.make_async_remote_copy(
+            src_ref=send.at[some], dst_ref=got.at[some], send_sem=s_sem, recv_sem=r_sem, device_id=me,
+            device_id_type=LOGICAL,
+        )
+
+    z = None
+    for i in range(4):
+        copies_of(send_f, recv_f, fwd_s, fwd_r.at[i], 64 if i < 3 else 63).wait_recv()
+        y4 = lax.rem(my_y + 4 - FAR[i], 4)
+        columns = pl.ds(pl.multiple_of(y4 * LANES, LANES), LANES)
+        high, low = halves(recv_f[pl.ds(y4 * 64, 64)].reshape(LANES, LANES))
+        both = dot(wide[pl.ds(2 * size, size), columns], jnp.concatenate([high, low], axis=1))
+        term = both[:, :LANES] + (both[:, LANES:] + dot(wide[pl.ds(3 * size, size), columns], high))
+        z = term if z is None else z + term
     z_re, z_im = z[:DEVICES], z[DEVICES:]
     cos, sin = twist[0][...], twist[1][...]
     turned = jnp.concatenate([z_re * cos + z_im * sin, z_im * cos - z_re * sin], axis=1)
@@ -361,37 +390,28 @@
     coarse_part = jnp.concatenate([xc_re * cos_c - xc_im * sin_c, xc_im * cos_c + xc_re * sin_c], axis=0)
     high, low = halves(jnp.concatenate([fine_part, coarse_part], axis=1))
 
-    def push_back(there, device):
+    def push_back(i, there, device):
         pltpu.make_async_remote_copy(
-            src_ref=send_i.at[there], dst_ref=recv_i.at[place], send_sem=inv_sem.at[0], recv_sem=inv_sem.at[1],
+            src_ref=send_i.at[there], dst_ref=recv_i.at[place], send_sem=inv_s, recv_sem=inv_r.at[i],
             device_id=device, device_id_type=LOGICAL,
         ).start()
 
     coarse_place = place // 2
 
-    def push_coarse(there, device):
+    def push_coarse(i, there, device):
         pltpu.make_async_remote_copy(
             src_ref=send_c.at[there], dst_ref=recv_c.at[coarse_place], send_sem=crs_sem.at[0],
             recv_sem=crs_sem.at[1], device_id=device, device_id_type=LOGICAL,
         ).start()
 
     for i in range(4):
-        y4 = lax.rem(my_y + (2, 1, 3, 0)[i], 4)
+        y4 = lax.rem(my_y + FAR[i], 4)
         upper = wide[pl.ds(4 * size + y4 * LANES, LANES)]
         lower = wide[pl.ds(5 * size + y4 * LANES, LANES)]
         planes = dot(upper, high) + (dot(upper, low) + dot(lower, high))
         send_i[pl.ds(y4 * 64, 64)] = planes[:, :LANES].reshape(64, 2, LANES)
         send_c[pl.ds(y4 * 64, 64)] = planes[:, LANES:].reshape(64, 2, LANES)
-
-        def one(j, carry, i=i):
-            for_column(i, j, push_back)
-            return carry
-
-        if i < 3:
-            lax.fori_loop(0, 4, one, 0)
-        else:
-            lax.fori_loop(0, 3, one, 0)
-            for_column(3, 3, push_back, ROWS - 1)
+        for_quarter(i, push_back)
     recv_i[place] = send_i[place]
 
     @pl.when(core == 0)
@@ -423,15 +443,17 @@
     for d in range(4):
         halo_wait(d, "source", put_source)
         halo_wait(d, "coarse", put_coarse)
-    kc[...] = jnp.zeros_like(kc)
-    arrived.wait_send()
-
-    returned = pltpu.make_async_remote_copy(
-        src_ref=send_i.at[many], dst_ref=recv_i.at[many], send_sem=inv_sem.at[0], recv_sem=inv_sem.at[1], device_id=me,
-        device_id_type=LOGICAL,
-    )
-    returned.wait_recv()
-    fine_log = table_right(recv_i[...].reshape(size, LANES).T, third_t)
+    copies_of(send_f, recv_f, fwd_s, fwd_r.at[0], DEVICES - 1).wait_send()
+
+    fine_log = None
+    for i in range(4):
+        copies_of(send_i, recv_i, inv_s, inv_r.at[i], 64 if i < 3 else 63).wait_recv()
+        y4 = lax.rem(my_y + 4 - FAR[i], 4)
+        high, low = halves(recv_i[pl.ds(y4 * 64, 64)].reshape(LANES, LANES).T)
+        upper, lower = wide[pl.ds(y4 * LANES, LANES)], wide[pl.ds(size + y4 * LANES, LANES)]
+        both = dot(jnp.concatenate([high, low], axis=0), upper)
+        term = both[:LANES] + (both[LANES:] + dot(high, lower))
+        fine_log = term if fine_log is None else fine_log + term
     fine_kappa = jnp.exp(fine_log).reshape(PB, QB, N2)
     for i, (dr, dc) in enumerate(DIRECTIONS[4:]):
         cor_s[i, 0] = fine_kappa[0 if dr < 0 else PB - 1, 0 if dc < 0 else QB - 1]
@@ -445,11 +467,7 @@
 
         @pl.when(core == own)
         def _(own=own):
-            some = pl.ds(0, 127 + own)
-            pltpu.make_async_remote_copy(
-                src_ref=recv_c.at[some], dst_ref=recv_c.at[some], send_sem=crs_sem.at[0], recv_sem=crs_sem.at[1],
-                device_id=me, device_id_type=LOGICAL,
-            ).wait_recv()
+            copies_of(recv_c, recv_c, crs_sem.at[0], crs_sem.at[1], 127 + own).wait_recv()
 
     coarse_log = table_right(recv_c[...].reshape(DEVICES, LANES).T, coarse_third)
     cell = lax.broadcasted_iota(jnp.int32, (LANES, half_n), 0)
@@ -459,20 +477,17 @@
     coarse_kappa = jnp.where(inside, jnp.exp(coarse_log), 0.0)
     for plane in range(CP):
         kc[plane, pl.ds(EDGE - 2, CQ)] = coarse_kappa[plane * CQ : (plane + 1) * CQ]
-    smooth(kc, fc, uc, coarse_out, half_p, half_q, half_n)
+    smooth(kc, fc, uc, coarse_out, half_p, half_q)
 
     for d in (0, 1, 2, 3, 4, 5, 6, 7):
         halo_wait(d, "kappa", put_kappa)
-    smooth(ke, fe, ue, fine_out, PB, QB, N2)
-
-    returned.wait_send()
+    smooth(ke, fe, ue, fine_out, PB, QB)
+
+    copies_of(send_i, recv_i, inv_s, inv_r.at[0], DEVICES - 1).wait_send()
 
     @pl.when(core == 0)
     def _():
-        pltpu.make_async_remote_copy(
-            src_ref=send_c.at[many], dst_ref=send_c.at[many], send_sem=crs_sem.at[0], recv_sem=crs_sem.at[1],
-            device_id=me, device_id_type=LOGICAL,
-        ).wait_send()
+        copies_of(send_c, send_c, crs_sem.at[0], crs_sem.at[1], DEVICES - 1).wait_send()
 
 
 def hand_over(fine, coarse, fine_out, coarse_out):
@@ -488,10 +503,7 @@
     sems = pltpu.SemaphoreType.DMA
     pressures = pl.pallas_call(
         kernel,
-        out_shape=(
-            jax.ShapeDtypeStruct((PB, QB, N2), F32),
-            jax.ShapeDtypeStruct((half_p, half_q, half_n), F32),
-        ),
+        out_shape=(pltpu.VMEM((PB, QB, N2), F32), pltpu.VMEM((half_p, half_q, half_n), F32)),
         in_specs=[anywhere] * 5,
         out_specs=(vmem, vmem),
         scratch_shapes=[pltpu.VMEM((PB, QB, N2), BF16)] * 2
@@ -508,7 +520,7 @@
         + [pltpu.VMEM((4, 1, N2), F32)] * 2
         + [pltpu.VMEM((2, PB, 1, N2), F32)] * 2
         + [pltpu.VMEM((2, half_p, 1, half_n), F32)] * 2
-        + [sems((6,)), sems((2,)), sems((2,)), sems((2,))]
+        + [sems((6,)), sems, sems((4,)), sems, sems((4,)), sems((2,))]
         + [sems((8,))] * 2
         + [sems((4,))] * 4,
         compiler_params=pltpu.CompilerParams(collective_id=0, has_side_effects=True, vmem_limit_bytes=VMEM_LIMIT),
@@ -518,6 +530,7 @@
         out_shape=tuple(jax.ShapeDtypeStruct(value.shape, value.dtype) for value in pressures),
         in_specs=[vmem] * 2,
         out_specs=(vmem, vmem),
+        compiler_params=pltpu.CompilerParams(vmem_limit_bytes=2 << 20),
     )(*pressures)
 
 

time: 45.1 us -> 42.9 us (0.951)
  Pallas kernels: 44.4 us -> 42.2 us
    pallas_call x1, Pallas kernels: 42.7 us -> 41.4 us  [body(): pl.pallas_call(kernel, out_shape=(pltpu.VMEM((PB, QB, N2), F32), pltpu.VM...]
    pallas_call x1, Pallas kernels: 1.68 us -> 0.72 us  [body(): pl.pallas_call(hand_over, out_shape=tuple((jax.ShapeDtypeStruct(value.sha...]
where the time goes in v3:
time: 42.9 us; the launch traced here: 42.8 us
  Pallas kernels  42.2 us (98%)
  between operations  0.64 us (1%)
    pallas_call x1, Pallas kernels, body(): pl.pallas_call(kernel, out_shape=(pltpu.VMEM((PB, QB, N2), F32), pltpu.VM...  41.4 us

profile of v3, /device:TPU:1, one launch (start us, length us, event | category | flops | bytes accessed | tf_op | source)
XLA Modules:
  0.0 42.8 jit_solution(11617575973979651847)
XLA Ops:
  0.6 41.4 %shard_map.68 = (f32[4,32,512]{2,1,0:T(8,128)S(1)}, f32[2,16,256]{2,1,0:T(8,128)S(1)}) custom-call(bf16[4,32,512]{2,1,0:T(8,128)(2,1)} %noise_h.1, bf16[4,32,512]{2,1,0:T(8,128)(2,1)} %source_h.1, bf16[3072,512]{1,0:T(8,128)(2,1)} %constant.6.clone.wide_h, bf16[2592,256]{1,0:T(8,128)(2,1)} %constant.7.clone.narrow_h, f32[7,256,128]{2,1,0:T(8,128)} %constant.8.clone.tables_h), custom_call_target="tpu_custom_call" | custom-call | tf_op jit(solution)/shard_map/pallas_call | solution.py:504
  42.1 0.7 %shard_map.69 = (f32[4,32,512]{2,1,0:T(8,128)}, f32[2,16,256]{2,1,0:T(8,128)}) custom-call(f32[4,32,512]{2,1,0:T(8,128)S(1)} %get-tuple-element.4.fine, f32[2,16,256]{2,1,0:T(8,128)S(1)} %get-tuple-element.5.coarse), custom_call_target="tpu_custom_call" | custom-call | tf_op jit(solution)/shard_map/pallas_call | solution.py:528

commit v4 on v3

--- a/solution.py
+++ b/solution.py
@@ -114,61 +114,57 @@
     return (c // 8) * 128 + r * 8 + c % 8
 
 
-def face_weight(center, beside):
-    return jnp.where(beside > 0.0, 0.5 * (center + beside), center)
-
-
-def beside_lanes(value, missing):
+def beside_lanes(value):
     depth = value.shape[-1]
     lane = lax.broadcasted_iota(jnp.int32, value.shape, 1)
-    after = jnp.where(lane == depth - 1, missing, pltpu.roll(value, depth - 1, 1))
-    before = jnp.where(lane == 0, missing, pltpu.roll(value, 1, 1))
+    after = jnp.where(lane == depth - 1, 0.0, pltpu.roll(value, depth - 1, 1))
+    before = jnp.where(lane == 0, 0.0, pltpu.roll(value, 1, 1))
     return after, before
 
 
-def first_sweep(center, neighbours, source):
-    diagonal = face_weight(center, neighbours[0])
-    for beside in neighbours[1:]:
-        diagonal = diagonal + face_weight(center, beside)
-    return JACOBI_WEIGHT * source / jnp.where(center > 0.0, diagonal, 1.0)
-
-
-def smooth(kappa, source, first, out, planes, width):
+def first_sweep(half, neighbours, source):
+    diagonal = 6.0 * half
+    for beside in neighbours:
+        diagonal = diagonal + jnp.where(beside > 0.0, beside, half)
+    return JACOBI_WEIGHT * source / jnp.where(half > 0.0, diagonal, 1.0), diagonal
+
+
+def smooth(halved, source, first, out, planes, width):
     mid, low, high = pl.ds(EDGE, width), pl.ds(EDGE - 1, width), pl.ds(EDGE + 1, width)
     for plane in range(planes + 2):
-        center = kappa[plane + 1, mid]
-        near = (kappa[plane + 2, mid], kappa[plane, mid], kappa[plane + 1, high], kappa[plane + 1, low])
-        first[plane, mid] = first_sweep(center, near + beside_lanes(center, 0.0), source[plane, mid])
+        half = halved[plane + 1, mid]
+        near = (halved[plane + 2, mid], halved[plane, mid], halved[plane + 1, high], halved[plane + 1, low])
+        value, diagonal = first_sweep(half, near + beside_lanes(half), source[plane, mid])
+        first[plane, mid] = value
+        if 1 <= plane <= planes:
+            out[plane - 1] = diagonal
     for at, inward, outward in ((EDGE - 1, EDGE, EDGE - 2), (EDGE + width, EDGE + width - 1, EDGE + width + 1)):
 
         def line(ref, base, q):
             return jnp.concatenate([ref[base + plane, pl.ds(q, 1)] for plane in range(planes)], axis=0)
 
-        center = line(kappa, 2, at)
-        near = (line(kappa, 3, at), line(kappa, 1, at), line(kappa, 2, inward), line(kappa, 2, outward))
-        value = first_sweep(center, near + beside_lanes(center, 0.0), line(source, 1, at))
+        half = line(halved, 2, at)
+        near = (line(halved, 3, at), line(halved, 1, at), line(halved, 2, inward), line(halved, 2, outward))
+        value, _ = first_sweep(half, near + beside_lanes(half), line(source, 1, at))
         for plane in range(planes):
             first[1 + plane, pl.ds(at, 1)] = value[plane : plane + 1]
     for plane in range(planes):
-        center = kappa[plane + 2, mid]
+        half = halved[plane + 2, mid]
         inner = first[plane + 1, mid]
-        total = jnp.zeros_like(center)
-        diagonal = jnp.zeros_like(center)
-        after, before = beside_lanes(center, 0.0)
-        after_value, before_value = beside_lanes(inner, 0.0)
+        diagonal = out[plane]
+        total = source[plane + 1, mid] - diagonal * inner
+        after, before = beside_lanes(half)
+        after_value, before_value = beside_lanes(inner)
         for beside, value in (
-            (kappa[plane + 3, mid], first[plane + 2, mid]),
-            (kappa[plane + 1, mid], first[plane, mid]),
-            (kappa[plane + 2, high], first[plane + 1, high]),
-            (kappa[plane + 2, low], first[plane + 1, low]),
+            (halved[plane + 3, mid], first[plane + 2, mid]),
+            (halved[plane + 1, mid], first[plane, mid]),
+            (halved[plane + 2, high], first[plane + 1, high]),
+            (halved[plane + 2, low], first[plane + 1, low]),
             (after, after_value),
             (before, before_value),
         ):
-            face = face_weight(center, beside)
-            diagonal = diagonal + face
-            total = total + face * value
-        residual = source[plane + 1, mid] - diagonal * inner + total
-        out[plane] = inner + JACOBI_WEIGHT * residual / diagonal
+            total = total + (half + jnp.where(beside > 0.0, beside, half)) * value
+        out[plane] = inner + JACOBI_WEIGHT * total / diagonal
 
 
 def kernel(
@@ -222,7 +218,6 @@
     def greet(i, there, device):
         pl.semaphore_signal(barrier, inc=1, device_id=device, device_id_type=LOGICAL)
 
-    for_all_peers(greet)
 
     size = 2 * DEVICES
     pairs = (
@@ -232,7 +227,10 @@
         (wide_h.at[pl.ds(2 * size, 4 * size)], wide.at[pl.ds(2 * size, 4 * size)]),
     )
     loads = [pltpu.make_async_copy(a, b, table_sem.at[i]) for i, (a, b) in enumerate(pairs)]
-    for load in loads:
+    for load in loads[:3]:
+        load.start()
+    for_all_peers(greet)
+    for load in loads[3:]:
         load.start()
 
     class Parts:
@@ -383,12 +381,9 @@
     y = table_right(turned, inner)
     x = table_right(y * jnp.concatenate([amp, amp], axis=1), inner_t)
     x_re, x_im = x[:, :LANES], x[:, LANES:]
-    xc = table_right(y * jnp.concatenate([amp_c, amp_c], axis=1), inner_c)
-    xc_re, xc_im = xc[:, :LANES], xc[:, LANES:]
-    cos_c, sin_c = twist_c[0][...], twist_c[1][...]
     fine_part = jnp.concatenate([x_re * cos - x_im * sin, x_im * cos + x_re * sin], axis=0)
-    coarse_part = jnp.concatenate([xc_re * cos_c - xc_im * sin_c, xc_im * cos_c + xc_re * sin_c], axis=0)
-    high, low = halves(jnp.concatenate([fine_part, coarse_part], axis=1))
+    high, low = halves(fine_part)
+    high_low = jnp.concatenate([high, low], axis=1)
 
     def push_back(i, there, device):
         pltpu.make_async_remote_copy(
@@ -408,15 +403,27 @@
         y4 = lax.rem(my_y + FAR[i], 4)
         upper = wide[pl.ds(4 * size + y4 * LANES, LANES)]
         lower = wide[pl.ds(5 * size + y4 * LANES, LANES)]
-        planes = dot(upper, high) + (dot(upper, low) + dot(lower, high))
-        send_i[pl.ds(y4 * 64, 64)] = planes[:, :LANES].reshape(64, 2, LANES)
-        send_c[pl.ds(y4 * 64, 64)] = planes[:, LANES:].reshape(64, 2, LANES)
+        both = dot(upper, high_low)
+        planes = both[:, :LANES] + (both[:, LANES:] + dot(lower, high))
+        send_i[pl.ds(y4 * 64, 64)] = planes.reshape(64, 2, LANES)
         for_quarter(i, push_back)
     recv_i[place] = send_i[place]
 
     @pl.when(core == 0)
     def _():
-        for_all_peers(push_coarse)
+        xc = table_right(y * jnp.concatenate([amp_c, amp_c], axis=1), inner_c)
+        xc_re, xc_im = xc[:, :LANES], xc[:, LANES:]
+        cos_c, sin_c = twist_c[0][...], twist_c[1][...]
+        high, low = halves(jnp.concatenate([xc_re * cos_c - xc_im * sin_c, xc_im * cos_c + xc_re * sin_c], axis=0))
+        high_low = jnp.concatenate([high, low], axis=1)
+        for i in range(4):
+            y4 = lax.rem(my_y + FAR[i], 4)
+            upper = wide[pl.ds(4 * size + y4 * LANES, LANES)]
+            lower = wide[pl.ds(5 * size + y4 * LANES, LANES)]
+            both = dot(upper, high_low)
+            planes = both[:, :LANES] + (both[:, LANES:] + dot(lower, high))
+            send_c[pl.ds(y4 * 64, 64)] = planes.reshape(64, 2, LANES)
+            for_quarter(i, push_coarse)
         recv_c[coarse_place] = send_c[place]
 
     def put_source(d):
@@ -454,12 +461,12 @@
         both = dot(jnp.concatenate([high, low], axis=0), upper)
         term = both[:LANES] + (both[LANES:] + dot(high, lower))
         fine_log = term if fine_log is None else fine_log + term
-    fine_kappa = jnp.exp(fine_log).reshape(PB, QB, N2)
+    fine_half = (0.5 * jnp.exp(fine_log)).reshape(PB, QB, N2)
     for i, (dr, dc) in enumerate(DIRECTIONS[4:]):
-        cor_s[i, 0] = fine_kappa[0 if dr < 0 else PB - 1, 0 if dc < 0 else QB - 1]
-    col_s[0] = fine_kappa[:, 0:2]
-    col_s[1] = fine_kappa[:, QB - 2 : QB]
-    ke[pl.ds(2, PB), mid] = fine_kappa
+        cor_s[i, 0] = fine_half[0 if dr < 0 else PB - 1, 0 if dc < 0 else QB - 1]
+    col_s[0] = fine_half[:, 0:2]
+    col_s[1] = fine_half[:, QB - 2 : QB]
+    ke[pl.ds(2, PB), mid] = fine_half
     for d in (4, 5, 6, 7, 2, 3, 0, 1):
         halo_start(d, "kappa")
 
@@ -474,9 +481,9 @@
     n0 = row * half_p + lax.div(cell, CQ) - 2
     n1 = group * half_q + lax.rem(cell, CQ) - 2
     inside = (n0 >= 0) & (n0 < N0 // 2) & (n1 >= 0) & (n1 < N1 // 2)
-    coarse_kappa = jnp.where(inside, jnp.exp(coarse_log), 0.0)
+    coarse_half = jnp.where(inside, 0.5 * jnp.exp(coarse_log), 0.0)
     for plane in range(CP):
-        kc[plane, pl.ds(EDGE - 2, CQ)] = coarse_kappa[plane * CQ : (plane + 1) * CQ]
+        kc[plane, pl.ds(EDGE - 2, CQ)] = coarse_half[plane * CQ : (plane + 1) * CQ]
     smooth(kc, fc, uc, coarse_out, half_p, half_q)
 
     for d in (0, 1, 2, 3, 4, 5, 6, 7):

time: 42.9 us -> 42.2 us (0.984)
  Pallas kernels: 42.2 us -> 41.5 us
    pallas_call x1, Pallas kernels: 41.4 us -> 40.8 us  [body(): pl.pallas_call(kernel, out_shape=(pltpu.VMEM((PB, QB, N2), F32), pltpu.VM...]
where the time goes in v4:
time: 42.2 us; the launch traced here: 42.1 us
  Pallas kernels  41.5 us (98%)
  between operations  0.64 us (2%)
    pallas_call x1, Pallas kernels, body(): pl.pallas_call(kernel, out_shape=(pltpu.VMEM((PB, QB, N2), F32), pltpu.VM...  40.8 us

profile of v4, /device:TPU:1, one launch (start us, length us, event | category | flops | bytes accessed | tf_op | source)
XLA Modules:
  0.0 42.1 jit_solution(962406924954810478)
XLA Ops:
  0.6 40.8 %shard_map.68 = (f32[4,32,512]{2,1,0:T(8,128)S(1)}, f32[2,16,256]{2,1,0:T(8,128)S(1)}) custom-call(bf16[4,32,512]{2,1,0:T(8,128)(2,1)} %noise_h.1, bf16[4,32,512]{2,1,0:T(8,128)(2,1)} %source_h.1, bf16[3072,512]{1,0:T(8,128)(2,1)} %constant.6.clone.wide_h, bf16[2592,256]{1,0:T(8,128)(2,1)} %constant.7.clone.narrow_h, f32[7,256,128]{2,1,0:T(8,128)} %constant.8.clone.tables_h), custom_call_target="tpu_custom_call" | custom-call | tf_op jit(solution)/shard_map/pallas_call | solution.py:511
  41.4 0.7 %shard_map.69 = (f32[4,32,512]{2,1,0:T(8,128)}, f32[2,16,256]{2,1,0:T(8,128)}) custom-call(f32[4,32,512]{2,1,0:T(8,128)S(1)} %get-tuple-element.4.fine, f32[2,16,256]{2,1,0:T(8,128)S(1)} %get-tuple-element.5.coarse), custom_call_target="tpu_custom_call" | custom-call | tf_op jit(solution)/shard_map/pallas_call | solution.py:535

commit v5 on v4

--- a/solution.py
+++ b/solution.py
@@ -266,8 +266,8 @@
     send_f[...] = spectrum.reshape(DEVICES, 2, LANES)
 
     fe[pl.ds(1, PB), pl.ds(EDGE, QB)] = source[...].astype(F32)
-    scol_s[0, :, 0] = source[:, 0].astype(F32)
-    scol_s[1, :, 0] = source[:, QB - 1].astype(F32)
+    scol_s[0, :, 0] = fe[pl.ds(1, PB), EDGE]
+    scol_s[1, :, 0] = fe[pl.ds(1, PB), EDGE + QB - 1]
 
     pl.semaphore_wait(barrier, DEVICES - 1)
 

time: 42.2 us -> 42.2 us (level)
  no operation moved by 1% of the time
where the time goes in v5:
time: 42.2 us; the launch traced here: 42.1 us
  Pallas kernels  41.5 us (98%)
  between operations  0.64 us (2%)
    pallas_call x1, Pallas kernels, body(): pl.pallas_call(kernel, out_shape=(pltpu.VMEM((PB, QB, N2), F32), pltpu.VM...  40.8 us

profile of v5, /device:TPU:1, one launch (start us, length us, event | category | flops | bytes accessed | tf_op | source)
XLA Modules:
  0.0 42.1 jit_solution(10871481710815918098)
XLA Ops:
  0.6 40.8 %shard_map.68 = (f32[4,32,512]{2,1,0:T(8,128)S(1)}, f32[2,16,256]{2,1,0:T(8,128)S(1)}) custom-call(bf16[4,32,512]{2,1,0:T(8,128)(2,1)} %noise_h.1, bf16[4,32,512]{2,1,0:T(8,128)(2,1)} %source_h.1, bf16[3072,512]{1,0:T(8,128)(2,1)} %constant.6.clone.wide_h, bf16[2592,256]{1,0:T(8,128)(2,1)} %constant.7.clone.narrow_h, f32[7,256,128]{2,1,0:T(8,128)} %constant.8.clone.tables_h), custom_call_target="tpu_custom_call" | custom-call | tf_op jit(solution)/shard_map/pallas_call | solution.py:511
  41.4 0.7 %shard_map.69 = (f32[4,32,512]{2,1,0:T(8,128)}, f32[2,16,256]{2,1,0:T(8,128)}) custom-call(f32[4,32,512]{2,1,0:T(8,128)S(1)} %get-tuple-element.4.fine, f32[2,16,256]{2,1,0:T(8,128)S(1)} %get-tuple-element.5.coarse), custom_call_target="tpu_custom_call" | custom-call | tf_op jit(solution)/shard_map/pallas_call | solution.py:535

commit v6 on v5

--- a/solution.py
+++ b/solution.py
@@ -126,18 +126,20 @@
     diagonal = 6.0 * half
     for beside in neighbours:
         diagonal = diagonal + jnp.where(beside > 0.0, beside, half)
-    return JACOBI_WEIGHT * source / jnp.where(half > 0.0, diagonal, 1.0), diagonal
-
-
-def smooth(halved, source, first, out, planes, width):
+    rate = JACOBI_WEIGHT / diagonal
+    return source * jnp.where(half > 0.0, rate, JACOBI_WEIGHT), diagonal, rate
+
+
+def smooth(halved, source, first, rates, out, planes, width):
     mid, low, high = pl.ds(EDGE, width), pl.ds(EDGE - 1, width), pl.ds(EDGE + 1, width)
     for plane in range(planes + 2):
         half = halved[plane + 1, mid]
         near = (halved[plane + 2, mid], halved[plane, mid], halved[plane + 1, high], halved[plane + 1, low])
-        value, diagonal = first_sweep(half, near + beside_lanes(half), source[plane, mid])
+        value, diagonal, rate = first_sweep(half, near + beside_lanes(half), source[plane, mid])
         first[plane, mid] = value
         if 1 <= plane <= planes:
             out[plane - 1] = diagonal
+            rates[plane - 1] = rate
     for at, inward, outward in ((EDGE - 1, EDGE, EDGE - 2), (EDGE + width, EDGE + width - 1, EDGE + width + 1)):
 
         def line(ref, base, q):
@@ -145,7 +147,7 @@
 
         half = line(halved, 2, at)
         near = (line(halved, 3, at), line(halved, 1, at), line(halved, 2, inward), line(halved, 2, outward))
-        value, _ = first_sweep(half, near + beside_lanes(half), line(source, 1, at))
+        value, _, _ = first_sweep(half, near + beside_lanes(half), line(source, 1, at))
         for plane in range(planes):
             first[1 + plane, pl.ds(at, 1)] = value[plane : plane + 1]
     for plane in range(planes):
@@ -164,14 +166,14 @@
             (before, before_value),
         ):
             total = total + (half + jnp.where(beside > 0.0, beside, half)) * value
-        out[plane] = inner + JACOBI_WEIGHT * total / diagonal
+        out[plane] = inner + total * rates[plane]
 
 
 def kernel(
     noise_h, source_h, wide_h, narrow_h, tables_h, fine_out, coarse_out,
     noise, source, wide, narrow, tables_v,
     send_f, recv_f, send_i, recv_i, send_c, recv_c,
-    ke, fe, ue, kc, fc, uc,
+    ke, fe, ue, kc, fc, uc, re, rc,
     col_s, col_r, cor_s, cor_r, scol_s, scol_r, cscol_s, cscol_r,
     table_sem, fwd_s, fwd_r, inv_s, inv_r, crs_sem, halo_s, halo_r, src_s, src_r, csrc_s, csrc_r,
 ):
@@ -484,11 +486,11 @@
     coarse_half = jnp.where(inside, 0.5 * jnp.exp(coarse_log), 0.0)
     for plane in range(CP):
         kc[plane, pl.ds(EDGE - 2, CQ)] = coarse_half[plane * CQ : (plane + 1) * CQ]
-    smooth(kc, fc, uc, coarse_out, half_p, half_q)
+    smooth(kc, fc, uc, rc, coarse_out, half_p, half_q)
 
     for d in (0, 1, 2, 3, 4, 5, 6, 7):
         halo_wait(d, "kappa", put_kappa)
-    smooth(ke, fe, ue, fine_out, PB, QB)
+    smooth(ke, fe, ue, re, fine_out, PB, QB)
 
     copies_of(send_i, recv_i, inv_s, inv_r.at[0], DEVICES - 1).wait_send()
 
@@ -522,6 +524,7 @@
             pltpu.VMEM((PB + 2, QB + 16, N2), F32),
             pltpu.VMEM((half_p + 4, half_q + 16, half_n), F32), pltpu.VMEM((half_p + 2, half_q + 16, half_n), F32),
             pltpu.VMEM((half_p + 2, half_q + 16, half_n), F32),
+            pltpu.VMEM((PB, QB, N2), F32), pltpu.VMEM((half_p, half_q, half_n), F32),
         ]
         + [pltpu.VMEM((2, PB, 2, N2), F32)] * 2
         + [pltpu.VMEM((4, 1, N2), F32)] * 2

time: 42.2 us -> 42.2 us (level)
  no operation moved by 1% of the time
where the time goes in v6:
time: 42.2 us; the launch traced here: 42.1 us
  Pallas kernels  41.5 us (98%)
  between operations  0.64 us (2%)
    pallas_call x1, Pallas kernels, body(): pl.pallas_call(kernel, out_shape=(pltpu.VMEM((PB, QB, N2), F32), pltpu.VM...  40.8 us

profile of v6, /device:TPU:1, one launch (start us, length us, event | category | flops | bytes accessed | tf_op | source)
XLA Modules:
  0.0 42.1 jit_solution(4700105815161438574)
XLA Ops:
  0.6 40.8 %shard_map.68 = (f32[4,32,512]{2,1,0:T(8,128)S(1)}, f32[2,16,256]{2,1,0:T(8,128)S(1)}) custom-call(bf16[4,32,512]{2,1,0:T(8,128)(2,1)} %noise_h.1, bf16[4,32,512]{2,1,0:T(8,128)(2,1)} %source_h.1, bf16[3072,512]{1,0:T(8,128)(2,1)} %constant.6.clone.wide_h, bf16[2592,256]{1,0:T(8,128)(2,1)} %constant.7.clone.narrow_h, f32[7,256,128]{2,1,0:T(8,128)} %constant.8.clone.tables_h), custom_call_target="tpu_custom_call" | custom-call | tf_op jit(solution)/shard_map/pallas_call | solution.py:513
  41.4 0.7 %shard_map.69 = (f32[4,32,512]{2,1,0:T(8,128)}, f32[2,16,256]{2,1,0:T(8,128)}) custom-call(f32[4,32,512]{2,1,0:T(8,128)S(1)} %get-tuple-element.4.fine, f32[2,16,256]{2,1,0:T(8,128)S(1)} %get-tuple-element.5.coarse), custom_call_target="tpu_custom_call" | custom-call | tf_op jit(solution)/shard_map/pallas_call | solution.py:538
